TPU v7x, 32 devices: a whole 2x2x4 slice. The times are simulated.
32 devices in a mesh: lon: 8 (over y, x, core), lat: 4 (over z).
Axes of the slice: x: 2, y: 2, z: 4, core: 2. Of those that a mesh axis runs over, the one named last changes fastest.
Arguments:
- state_prev: float32 [7, 16, 64, 1024], P(None, None, 'lat', 'lon'), may hold values from -6 to 6
- state_now: float32 [7, 16, 64, 1024], P(None, None, 'lat', 'lon'), may hold values from -6 to 6
- stride_table: int32 [64], P('lat'), may hold values from 1 to 32, as said below
- filter_len: int32 [64], P('lat'), may hold values from 1 to 32, as said below
- zonal_coef: float32 [64], P('lat'), may hold values from 0.05 to 0.3
- merid_coef: float32 [16], replicated, may hold values from 0.05 to 0.3
- filter_coef: float32 [16], replicated, may hold values from 0.03 to 0.2
- w_first: bfloat16 [7, 64], replicated, may hold values from -2 to 2
- b_first: float32 [64], replicated, may hold values from -3 to 3
- w_second: bfloat16 [64, 64], replicated, may hold values from -0.75 to 0.75
- b_second: float32 [64], replicated, may hold values from -3 to 3
- w_third: bfloat16 [64, 224], replicated, may hold values from -0.75 to 0.75
- b_third: float32 [224], replicated, may hold values from -3 to 3
- band_weight: float32 [224], replicated, may hold values from 0.02 to 0.2
- sunlit_cols: int32 [4, 8, 1536], P('lat', 'lon'), may hold values from 0 to 2047, as said below
- sunlit_count: int32 [4, 8], P('lat'), may hold values from 0 to 1536, as said below
Outputs:
- prev_out: float32 [7, 16, 64, 1024], P(None, None, 'lat', 'lon')
- now_out: float32 [7, 16, 64, 1024], P(None, None, 'lat', 'lon')
Inputs may be any that keep to these rules, and one draw needn't show every extreme that they name: `stride_table`: 1 except in the 4 rows nearest each end of the latitude range. `filter_len`: 1 except in the 4 rows nearest each end of the latitude range. `sunlit_cols`: the entries of one device's list are distinct. `sunlit_count`: a device's count plus that of the device 8 / 2 further along lon (cyclic) in the same band is at most 1536.
All inputs are finite; a program needn't handle non-finite values.
Results may differ from a plain program's by a relative error of at most 0.0003.
Values may be sent and summed in bfloat16 or wider, within the bound.
A program may use at most 64 MiB of HBM per device.

v0:
```python
import jax
import jax.numpy as jnp
from jax import lax
from jax.sharding import PartitionSpec as P

SMAX = 32
POLAR = 4
BLK = 128


def extended(cells, sides, width, closed):
    for axis, dim in sides:
        count = lax.axis_size(axis)
        ends = count if closed else count - 1
        head = lax.slice_in_dim(cells, 0, width, axis=dim)
        tail = lax.slice_in_dim(cells, cells.shape[dim] - width, cells.shape[dim], axis=dim)
        cells = jnp.concatenate(
            [
                lax.ppermute(tail, axis, [(i, (i + 1) % count) for i in range(ends)]),
                cells,
                lax.ppermute(head, axis, [((i + 1) % count, i) for i in range(ends)]),
            ],
            axis=dim,
        )
    return cells


def shifted_2(block, axis, distance):
    devices = range(lax.axis_size(axis))
    route = [((i - distance) % len(devices), i) for i in devices]
    return lax.ppermute(block, axis, route)


def absorb(feats_t, w_first, b_first, w_second, b_second, w_third, b_third, band_weight):
    count = feats_t.shape[2]
    levels = feats_t.shape[1]
    rows = jnp.transpose(feats_t, (2, 1, 0)).reshape(count * levels, feats_t.shape[0])
    first = jax.nn.silu(
        jnp.dot(rows, w_first, preferred_element_type=jnp.float32) + b_first
    ).astype(jnp.bfloat16)
    second = jax.nn.silu(
        jnp.dot(first, w_second, preferred_element_type=jnp.float32) + b_second
    ).astype(jnp.bfloat16)
    tau = 0.15 * jax.nn.softplus(
        jnp.dot(second, w_third, preferred_element_type=jnp.float32) + b_third
    )
    tau = tau.reshape(count, levels, tau.shape[-1])
    depth = jnp.cumsum(tau, axis=1)
    above = depth - tau
    return jnp.sum((jnp.exp(-above) - jnp.exp(-depth)) * band_weight, axis=-1)


def network(feats_t, weights):
    groups = feats_t.shape[2] // BLK
    blocks = jnp.moveaxis(feats_t.reshape(feats_t.shape[0], feats_t.shape[1], groups, BLK), 2, 0)
    heats = lax.map(lambda block: absorb(block, *weights), blocks)
    return heats.reshape(groups * BLK, feats_t.shape[1])


def shifted(center, offsets, sign, pstart, width):
    static = center[:, :, :, SMAX + sign : SMAX + sign + width]
    pieces = []
    for place in range(POLAR):
        row_at = pstart + place
        row = lax.dynamic_index_in_dim(center, row_at, 2, False)
        start = SMAX + sign * offsets[row_at]
        pieces.append(lax.dynamic_slice_in_dim(row, start, width, 2))
    slab = jnp.stack(pieces, axis=2)
    return lax.dynamic_update_slice_in_dim(static, slab, pstart, 2)


def tendency(center, merid, stride, flen, zcoef, merid_coef, filter_coef, pstart, width):
    field = center[:, :, :, SMAX : SMAX + width]
    inv_s = 1.0 / stride.astype(jnp.float32)
    plus = shifted(center, stride, 1, pstart, width)
    minus = shifted(center, stride, -1, pstart, width)
    fplus = shifted(center, flen, 1, pstart, width)
    fminus = shifted(center, flen, -1, pstart, width)
    wind_u = field[0][None]
    wind_v = field[1][None]
    tend = -zcoef[None, None, :, None] * wind_u * ((plus - minus) * inv_s[None, None, :, None])
    tend = tend - merid_coef[None, :, None, None] * wind_v * merid
    tend = tend + filter_coef[None, :, None, None] * (fplus - 2.0 * field + fminus)
    return tend


def polar_start(rows):
    return jnp.where(lax.axis_index("lat") == 0, 0, rows - POLAR).astype(jnp.int32)


def zonal_cells(now):
    return extended(now, (("lon", 3),), SMAX, True)


def leap(prev, now, stride_table, filter_len, zonal_coef, merid_coef, filter_coef):
    wide = zonal_cells(now)
    banded = extended(now, (("lat", 2),), 1, False)
    merid = banded[:, :, 2:] - banded[:, :, :-2]
    pstart = polar_start(now.shape[2])
    tend = tendency(
        wide,
        merid,
        stride_table,
        filter_len,
        zonal_coef,
        merid_coef,
        filter_coef,
        pstart,
        now.shape[3],
    )
    new = prev + tend
    return (now + 0.1 * (prev - 2.0 * now + new), new)


def body(
    state_prev,
    state_now,
    stride_table,
    filter_len,
    zonal_coef,
    merid_coef,
    filter_coef,
    w_first,
    b_first,
    w_second,
    b_second,
    w_third,
    b_third,
    band_weight,
    sunlit_cols,
    sunlit_count,
):
    prev, now = (state_prev, state_now)
    for turn in range(2):
        prev, now = leap(prev, now, stride_table, filter_len, zonal_coef, merid_coef, filter_coef)
    weights = (w_first, b_first, w_second, b_second, w_third, b_third, band_weight)
    cells = now.shape[2] * now.shape[3]
    flat = now.reshape(now.shape[0], now.shape[1], cells)
    listed = sunlit_cols.reshape(-1)
    slots_all = listed.shape[0]
    feats_t = jnp.take(flat, listed, axis=2).astype(jnp.bfloat16)
    lon_here = lax.axis_index("lon")
    lon_count = lax.axis_size("lon")
    counts_row = sunlit_count.reshape(-1)
    mine = counts_row[lon_here]
    half = slots_all // 2
    other = counts_row[(lon_here + lon_count // 2) % lon_count]
    excess = feats_t[:, :, half:]
    arrived = shifted_2(excess, "lon", lon_count // 2)
    slots = jnp.arange(half, dtype=jnp.int32)
    place = jnp.clip(slots - mine, 0, half - 1)
    buffer = jnp.where(
        (slots < mine)[None, None, :], feats_t[:, :, :half], jnp.take(arrived, place, axis=2)
    )
    computed = network(buffer, weights)
    over_other = jnp.maximum(other - half, 0)
    back_index = jnp.clip(mine + slots, 0, half - 1)
    outgoing = jnp.where((slots < over_other)[:, None], computed[back_index], jnp.float32(0.0))
    returned = shifted_2(outgoing.T, "lon", lon_count // 2)
    own = jnp.where((slots < mine)[:, None], computed, jnp.float32(0.0))
    heat = jnp.concatenate([own, returned.T], axis=0)
    temper = now[2].reshape(now.shape[1], cells).at[:, listed].add(heat.T)
    now_out = now.at[2].set(temper.reshape(now.shape[1], now.shape[2], now.shape[3]))
    return (prev, now_out)


def solution(mesh):
    in_specs = (
        P(None, None, "lat", "lon"),
        P(None, None, "lat", "lon"),
        P("lat"),
        P("lat"),
        P("lat"),
        P(),
        P(),
        P(),
        P(),
        P(),
        P(),
        P(),
        P(),
        P(),
        P("lat", "lon", None),
        P("lat", None),
    )
    out_specs = (P(None, None, "lat", "lon"), P(None, None, "lat", "lon"))
    return jax.shard_map(body, mesh=mesh, in_specs=in_specs, out_specs=out_specs, check_vma=False)
```

profile of v0, /device:TPU:0, one launch (start us, length us, event | category | flops | bytes accessed | tf_op | source)
XLA Modules:
  0.0 206.7 jit_solution(11165705636662846626)
XLA Ops:
  0.7 3.0 %fusion.32 = (f32[7,16,16,32]{3,2,1,0:T(8,128)}, f32[7,16,16,32]{3,2,1,0:T(8,128)}) fusion(f32[7,16,16,128]{3,2,1,0:T(8,128)} %param.21), kind=kLoop, calls=%fused_computation.119 | loop fusion | bytes 917504 | tf_op jit(solution)/shard_map/slice | solution.py:15
  3.8 3.3 %collective-permute-start = (f32[7,16,16,32]{3,2,1,0:T(8,128)}, f32[7,16,16,32]{3,2,1,0:T(8,128)S(1)}, u32[]{:S(2)}, u32[]{:S(2)}) collective-permute-start(f32[7,16,16,32]{3,2,1,0:T(8,128)} %get-tuple-element.163), channel_id=1, source_target_pairs={{4,0},{8,4},{12,8},{16,12},{20,16},{24,20},{28,24},{0,28},{5,1},{9... | collective-permute-start | bytes 688136 | tf_op jit(solution)/shard_map/ppermute | solution.py:21
  8.5 4.5 %collective-permute-start.3 = (f32[7,16,1,128]{3,2,1,0:T(1,128)S(1)}, f32[7,16,1,128]{3,2,1,0:T(1,128)S(1)}, u32[]{:S(2)}, u32[]{:S(2)}) collective-permute-start(f32[7,16,1,128]{3,2,1,0:T(1,128)S(1)} %get-tuple-element.166), channel_id=1, source_target_pairs={{0,1},{1,2},{2,3},{4,5},{5,6},{6,7},{8,9},{9,10},{10,11},{12,13},{... | collective-permute-start | bytes 172040 | tf_op jit(solution)/shard_map/ppermute | solution.py:19
  43.9 4.7 %collective-permute-start.7 = (f32[7,16,1,128]{3,2,1,0:T(1,128)S(1)}, f32[7,16,1,128]{3,2,1,0:T(1,128)S(1)}, u32[]{:S(2)}, u32[]{:S(2)}) collective-permute-start(f32[7,16,1,128]{3,2,1,0:T(1,128)S(1)} %get-tuple-element.154), channel_id=1, source_target_pairs={{0,1},{1,2},{2,3},{4,5},{5,6},{6,7},{8,9},{9,10},{10,11},{12,13},{... | collective-permute-start | bytes 172040 | tf_op jit(solution)/shard_map/ppermute | solution.py:19
  48.8 12.8 %collective-permute-done.4 = f32[7,16,16,32]{3,2,1,0:T(8,128)S(1)} collective-permute-done((f32[7,16,16,32]{3,2,1,0:T(8,128)S(1)}, f32[7,16,16,32]{3,2,1,0:T(8,128)S(1)}, u32[]{:S(2)}, u32[]{:S(2)}) %collective-permute-start.4) | collective-permute-done | bytes 229408 | tf_op jit(solution)/shard_map/ppermute | solution.py:21
  71.5 4.0 %copy.54 = bf16[7,16,16,128]{1,0,3,2:T(8,128)(2,1)} copy(f32[7,16,16,128]{3,2,1,0:T(8,128)S(1)} %get-tuple-element.118) | data formatting | bytes 1376256 | tf_op jit(solution)/shard_map/add | solution.py:111
  75.4 6.0 %gather_fusion = bf16[1536,7,16]{2,1,0:T(8,128)(2,1)} fusion(bf16[7,16,2048]{1,0,2:T(8,128)(2,1)} %bitcast.93, s32[2048]{0:T(1024)S(1)} %pad_clamp_fusion), kind=kCustom, calls=%fused_computation | custom fusion | bytes 694272 | tf_op jit(solution)/shard_map/jit(_take)/gather | solution.py:141
  81.5 8.0 %fusion.6 = bf16[7,16,1536]{1,0,2:T(8,128)(2,1)S(1)} fusion(bf16[1536,7,16]{2,1,0:T(8,128)(2,1)} %gather_fusion, pred[1536]{0:T(1024)(128)(4,1)S(1)} %compare_and_fusion), kind=kLoop, calls=%fused_computation.20 | loop fusion | flops 172032 | bytes 689664 | tf_op jit(solution)/shard_map/convert_element_type | solution.py:141
  98.7 3.2 %gather_fusion.1 = bf16[768,7,16]{2,1,0:T(8,128)(2,1)} fusion(bf16[7,16,768]{1,0,2:T(8,128)(2,1)S(1)} %copy.56, s32[1024]{0:T(1024)S(1)} %pad_clamp_fusion.2), kind=kCustom, calls=%fused_computation.1 | custom fusion | bytes 347136 | tf_op jit(solution)/shard_map/jit(_take)/gather | solution.py:153
  101.8 6.5 %slice_select_fusion = bf16[7,16,768]{1,0,2:T(8,128)(2,1)S(1)} fusion(bf16[7,16,1536]{1,0,2:T(8,128)(2,1)} %copy-done.1, bf16[768,7,16]{2,1,0:T(8,128)(2,1)} %gather_fusion.1, pred[768]{0:T(1024)(128)(4,1)S(1)} %get-tuple-element.182, pred[768]{0:T(1024)(128)(4,1)S(1)} %get-tuple-element.181), kind=kLoop, calls=%fused_computation.23 | loop fusion | flops 172032 | bytes 517632 | tf_op jit(solution)/shard_map/jit(_where)/select_n | solution.py:152
  109.2 77.9 %while.11 = (s32[]{:T(128)}, f32[6,128,16]{2,1,0:T(8,128)S(1)}, bf16[6,7,16,128]{2,3,1,0:T(8,128)(2,1)S(1)}, bf16[7,64]{1,0:T(8,128)(2,1)S(1)}, f32[64]{0:T(128)...) while((s32[]{:T(128)}, f32[6,128,16]{2,1,0:T(8,128)S(1)}, ...), condition=%wide.region_3.4_spmd, body=%wide.region_0.3_spmd.sunk | while | flops 92207104 | bytes 22424876 | solution.py:56
  110.3 2.7 %fusion.55 = f32[2048,224]{0,1:T(8,128)} fusion(bf16[64,224]{1,0:T(8,128)(2,1)S(1)} %get-tuple-element.273, f32[224]{0:T(256)S(1)} %get-tuple-element.274, bf16[2048,64]{0,1:T(8,128)(2,1)S(1)} %multiply_convert_fusion.3, bf16[64,64]{1,0:T(8,128)(2,1)S(1)} %get-tuple-element.271, f32[64]{0:T(128)S(1)} %get-tuple-element.272), kind=kOutput, calls=%fused_computation.10.clone.1 | convolution fusion | flops 79953920 | bytes 2135168 | tf_op jit(solution)/shard_map/while/body/eval_jaxpr/dot_general | solution.py:45
  119.3 2.8 %multiply_reduce_fusion.2 = f32[2048]{0:T(1024)S(1)} fusion(f32[2048,224]{0,1:T(8,128)} %copy.71, f32[2048,224]{0,1:T(8,128)} %fusion.55, f32[224]{0:T(256)S(1)} %get-tuple-element.275), kind=kLoop, calls=%fused_computation.11.clone.1 | loop fusion | flops 2750464 | bytes 3679104 | tf_op jit(solution)/shard_map/while/body/eval_jaxpr/reduce_sum | solution.py:50
  123.3 2.7 %fusion.55 = f32[2048,224]{0,1:T(8,128)} fusion(bf16[64,224]{1,0:T(8,128)(2,1)S(1)} %get-tuple-element.273, f32[224]{0:T(256)S(1)} %get-tuple-element.274, bf16[2048,64]{0,1:T(8,128)(2,1)S(1)} %multiply_convert_fusion.3, bf16[64,64]{1,0:T(8,128)(2,1)S(1)} %get-tuple-element.271, f32[64]{0:T(128)S(1)} %get-tuple-element.272), kind=kOutput, calls=%fused_computation.10.clone.1 | convolution fusion | flops 79953920 | bytes 2135168 | tf_op jit(solution)/shard_map/while/body/eval_jaxpr/dot_general | solution.py:45
  132.2 2.8 %multiply_reduce_fusion.2 = f32[2048]{0:T(1024)S(1)} fusion(f32[2048,224]{0,1:T(8,128)} %copy.71, f32[2048,224]{0,1:T(8,128)} %fusion.55, f32[224]{0:T(256)S(1)} %get-tuple-element.275), kind=kLoop, calls=%fused_computation.11.clone.1 | loop fusion | flops 2750464 | bytes 3679104 | tf_op jit(solution)/shard_map/while/body/eval_jaxpr/reduce_sum | solution.py:50
  136.3 2.7 %fusion.55 = f32[2048,224]{0,1:T(8,128)} fusion(bf16[64,224]{1,0:T(8,128)(2,1)S(1)} %get-tuple-element.273, f32[224]{0:T(256)S(1)} %get-tuple-element.274, bf16[2048,64]{0,1:T(8,128)(2,1)S(1)} %multiply_convert_fusion.3, bf16[64,64]{1,0:T(8,128)(2,1)S(1)} %get-tuple-element.271, f32[64]{0:T(128)S(1)} %get-tuple-element.272), kind=kOutput, calls=%fused_computation.10.clone.1 | convolution fusion | flops 79953920 | bytes 2135168 | tf_op jit(solution)/shard_map/while/body/eval_jaxpr/dot_general | solution.py:45
  145.2 2.8 %multiply_reduce_fusion.2 = f32[2048]{0:T(1024)S(1)} fusion(f32[2048,224]{0,1:T(8,128)} %copy.71, f32[2048,224]{0,1:T(8,128)} %fusion.55, f32[224]{0:T(256)S(1)} %get-tuple-element.275), kind=kLoop, calls=%fused_computation.11.clone.1 | loop fusion | flops 2750464 | bytes 3679104 | tf_op jit(solution)/shard_map/while/body/eval_jaxpr/reduce_sum | solution.py:50
  158.2 2.8 %multiply_reduce_fusion.2 = f32[2048]{0:T(1024)S(1)} fusion(f32[2048,224]{0,1:T(8,128)} %copy.71, f32[2048,224]{0,1:T(8,128)} %fusion.55, f32[224]{0:T(256)S(1)} %get-tuple-element.275), kind=kLoop, calls=%fused_computation.11.clone.1 | loop fusion | flops 2750464 | bytes 3679104 | tf_op jit(solution)/shard_map/while/body/eval_jaxpr/reduce_sum | solution.py:50
  162.2 2.7 %fusion.55 = f32[2048,224]{0,1:T(8,128)} fusion(bf16[64,224]{1,0:T(8,128)(2,1)S(1)} %get-tuple-element.273, f32[224]{0:T(256)S(1)} %get-tuple-element.274, bf16[2048,64]{0,1:T(8,128)(2,1)S(1)} %multiply_convert_fusion.3, bf16[64,64]{1,0:T(8,128)(2,1)S(1)} %get-tuple-element.271, f32[64]{0:T(128)S(1)} %get-tuple-element.272), kind=kOutput, calls=%fused_computation.10.clone.1 | convolution fusion | flops 79953920 | bytes 2135168 | tf_op jit(solution)/shard_map/while/body/eval_jaxpr/dot_general | solution.py:45
  171.2 2.8 %multiply_reduce_fusion.2 = f32[2048]{0:T(1024)S(1)} fusion(f32[2048,224]{0,1:T(8,128)} %copy.71, f32[2048,224]{0,1:T(8,128)} %fusion.55, f32[224]{0:T(256)S(1)} %get-tuple-element.275), kind=kLoop, calls=%fused_computation.11.clone.1 | loop fusion | flops 2750464 | bytes 3679104 | tf_op jit(solution)/shard_map/while/body/eval_jaxpr/reduce_sum | solution.py:50
  175.2 2.7 %fusion.55 = f32[2048,224]{0,1:T(8,128)} fusion(bf16[64,224]{1,0:T(8,128)(2,1)S(1)} %get-tuple-element.273, f32[224]{0:T(256)S(1)} %get-tuple-element.274, bf16[2048,64]{0,1:T(8,128)(2,1)S(1)} %multiply_convert_fusion.3, bf16[64,64]{1,0:T(8,128)(2,1)S(1)} %get-tuple-element.271, f32[64]{0:T(128)S(1)} %get-tuple-element.272), kind=kOutput, calls=%fused_computation.10.clone.1 | convolution fusion | flops 79953920 | bytes 2135168 | tf_op jit(solution)/shard_map/while/body/eval_jaxpr/dot_general | solution.py:45
  184.2 2.8 %multiply_reduce_fusion.2 = f32[2048]{0:T(1024)S(1)} fusion(f32[2048,224]{0,1:T(8,128)} %copy.71, f32[2048,224]{0,1:T(8,128)} %fusion.55, f32[224]{0:T(256)S(1)} %get-tuple-element.275), kind=kLoop, calls=%fused_computation.11.clone.1 | loop fusion | flops 2750464 | bytes 3679104 | tf_op jit(solution)/shard_map/while/body/eval_jaxpr/reduce_sum | solution.py:50
  189.6 7.1 %collective-permute-done.9 = f32[16,768]{0,1:T(8,128)S(1)} collective-permute-done((f32[16,768]{0,1:T(8,128)S(1)}, f32[16,768]{0,1:T(8,128)S(1)}, u32[]{:S(2)}, u32[]{:S(2)}) %collective-permute-start.9) | collective-permute-done | bytes 49184 | tf_op jit(solution)/shard_map/ppermute | solution.py:31
  196.7 9.0 %scatter_custom_fusion = f32[16,2048]{0,1:T(8,128)S(1)} fusion(f32[16,2048]{0,1:T(8,128)S(1)} %bitcast.94, s32[1536]{0:T(1024)S(1)} %fusion.23, f32[768,16]{1,0:T(8,128)S(1)} %bitcast.96, f32[]{:T(128)} %constant.918, f32[768,16]{1,0:T(8,128)S(1)} %broadcast_select_fusion), kind=kCustom, calls=%fused_computation.44 | custom fusion | flops 49152 | bytes 917508 | tf_op jit(solution)/shard_map/scatter-add | solution.py:162
  (184 shorter events, 86.5 us)
Async XLA Ops:
  0.6 6.5 %copy-start = (f32[7,16,16,128]{3,2,1,0:T(8,128)S(1)}, f32[7,16,16,128]{3,2,1,0:T(8,128)}, u32[]{:S(2)}) copy-start(f32[7,16,16,128]{3,2,1,0:T(8,128)} %param.21) | copy-start | bytes 2752516
  0.6 12.4 %copy-start.10 = (s32[16]{0:T(128)S(1)}, s32[16]{0:T(128)}, u32[]{:S(2)}) copy-start(s32[16]{0:T(128)} %param.22) | copy-start | bytes 196
  0.7 15.5 %copy-start.9 = (s32[16]{0:T(128)S(1)}, s32[16]{0:T(128)}, u32[]{:S(2)}) copy-start(s32[16]{0:T(128)} %param.23) | copy-start | bytes 196
  0.7 28.7 %copy-start.8 = (s32[1,1,1536]{2,1,0:T(1,128)S(1)}, s32[1,1,1536]{2,1,0:T(1,128)}, u32[]{:S(2)}) copy-start(s32[1,1,1536]{2,1,0:T(1,128)} %param.34) | copy-start | bytes 18436
  0.7 28.8 %copy-start.12 = (s32[1,8]{1,0:T(1,128)S(1)}, s32[1,8]{1,0:T(1,128)}, u32[]{:S(2)}) copy-start(s32[1,8]{1,0:T(1,128)} %param.35) | copy-start | bytes 100
  0.7 31.8 %copy-start.18 = (f32[16]{0:T(128)S(1)}, f32[16]{0:T(128)}, u32[]{:S(2)}) copy-start(f32[16]{0:T(128)} %param.24) | copy-start | bytes 196
  0.7 32.4 %copy-start.13 = (f32[16]{0:T(128)S(1)}, f32[16]{0:T(128)}, u32[]{:S(2)}) copy-start(f32[16]{0:T(128)} %param.25) | copy-start | bytes 196
  3.8 29.5 %collective-permute-start = (f32[7,16,16,32]{3,2,1,0:T(8,128)}, f32[7,16,16,32]{3,2,1,0:T(8,128)S(1)}, u32[]{:S(2)}, u32[]{:S(2)}) collective-permute-start(f32[7,16,16,32]{3,2,1,0:T(8,128)} %get-tuple-element.163), channel_id=1, source_target_pairs={{4,0},{8,4},{12,8},{16,12},{20,16},{24,20},{28,24},{0,28},{5,1},{9... | collective-permute-start | bytes 688136 | tf_op jit(solution)/shard_map/ppermute | solution.py:21
  7.1 26.1 %collective-permute-start.1 = (f32[7,16,16,32]{3,2,1,0:T(8,128)}, f32[7,16,16,32]{3,2,1,0:T(8,128)S(1)}, u32[]{:S(2)}, u32[]{:S(2)}) collective-permute-start(f32[7,16,16,32]{3,2,1,0:T(8,128)} %get-tuple-element.164), channel_id=1, source_target_pairs={{0,4},{4,8},{8,12},{12,16},{16,20},{20,24},{24,28},{28,0},{1,5},{5... | collective-permute-start | bytes 688136 | tf_op jit(solution)/shard_map/ppermute | solution.py:19
  7.2 32.1 %collective-permute-start.2 = (f32[7,16,1,128]{3,2,1,0:T(1,128)S(1)}, f32[7,16,1,128]{3,2,1,0:T(1,128)S(1)}, u32[]{:S(2)}, u32[]{:S(2)}) collective-permute-start(f32[7,16,1,128]{3,2,1,0:T(1,128)S(1)} %get-tuple-element.165), channel_id=1, source_target_pairs={{1,0},{2,1},{3,2},{5,4},{6,5},{7,6},{9,8},{10,9},{11,10},{13,12},{... | collective-permute-start | bytes 172040 | tf_op jit(solution)/shard_map/ppermute | solution.py:21
  8.5 30.8 %collective-permute-start.3 = (f32[7,16,1,128]{3,2,1,0:T(1,128)S(1)}, f32[7,16,1,128]{3,2,1,0:T(1,128)S(1)}, u32[]{:S(2)}, u32[]{:S(2)}) collective-permute-start(f32[7,16,1,128]{3,2,1,0:T(1,128)S(1)} %get-tuple-element.166), channel_id=1, source_target_pairs={{0,1},{1,2},{2,3},{4,5},{5,6},{6,7},{8,9},{9,10},{10,11},{12,13},{... | collective-permute-start | bytes 172040 | tf_op jit(solution)/shard_map/ppermute | solution.py:19
  35.2 4.1 %copy-start.6 = (f32[7,16,16,128]{3,2,1,0:T(8,128)S(1)}, f32[7,16,16,128]{3,2,1,0:T(8,128)}, u32[]{:S(2)}) copy-start(f32[7,16,16,128]{3,2,1,0:T(8,128)} %param.20) | copy-start | bytes 2752516
  35.2 4.1 %copy-start.11 = (f32[16]{0:T(128)S(1)}, f32[16]{0:T(128)}, u32[]{:S(2)}) copy-start(f32[16]{0:T(128)} %param.26) | copy-start | bytes 196
  40.5 21.0 %collective-permute-start.4 = (f32[7,16,16,32]{3,2,1,0:T(8,128)S(1)}, f32[7,16,16,32]{3,2,1,0:T(8,128)S(1)}, u32[]{:S(2)}, u32[]{:S(2)}) collective-permute-start(f32[7,16,16,32]{3,2,1,0:T(8,128)S(1)} %get-tuple-element.157), channel_id=1, source_target_pairs={{4,0},{8,4},{12,8},{16,12},{20,16},{24,20},{28,24},{0,28},{5,1},{9... | collective-permute-start | bytes 688136 | tf_op jit(solution)/shard_map/ppermute | solution.py:21
  42.6 20.9 %collective-permute-start.5 = (f32[7,16,16,32]{3,2,1,0:T(8,128)S(1)}, f32[7,16,16,32]{3,2,1,0:T(8,128)S(1)}, u32[]{:S(2)}, u32[]{:S(2)}) collective-permute-start(f32[7,16,16,32]{3,2,1,0:T(8,128)S(1)} %get-tuple-element.158), channel_id=1, source_target_pairs={{0,4},{4,8},{8,12},{12,16},{16,20},{20,24},{24,28},{28,0},{1,5},{5... | collective-permute-start | bytes 688136 | tf_op jit(solution)/shard_map/ppermute | solution.py:19
  42.6 26.9 %collective-permute-start.6 = (f32[7,16,1,128]{3,2,1,0:T(1,128)S(1)}, f32[7,16,1,128]{3,2,1,0:T(1,128)S(1)}, u32[]{:S(2)}, u32[]{:S(2)}) collective-permute-start(f32[7,16,1,128]{3,2,1,0:T(1,128)S(1)} %get-tuple-element.153), channel_id=1, source_target_pairs={{1,0},{2,1},{3,2},{5,4},{6,5},{7,6},{9,8},{10,9},{11,10},{13,12},{... | collective-permute-start | bytes 172040 | tf_op jit(solution)/shard_map/ppermute | solution.py:21
  43.9 25.7 %collective-permute-start.7 = (f32[7,16,1,128]{3,2,1,0:T(1,128)S(1)}, f32[7,16,1,128]{3,2,1,0:T(1,128)S(1)}, u32[]{:S(2)}, u32[]{:S(2)}) collective-permute-start(f32[7,16,1,128]{3,2,1,0:T(1,128)S(1)} %get-tuple-element.154), channel_id=1, source_target_pairs={{0,1},{1,2},{2,3},{4,5},{5,6},{6,7},{8,9},{9,10},{10,11},{12,13},{... | collective-permute-start | bytes 172040 | tf_op jit(solution)/shard_map/ppermute | solution.py:19
  71.5 10.0 %copy-start.4 = (f32[7,16,16,128]{3,2,1,0:T(8,128)}, f32[7,16,16,128]{3,2,1,0:T(8,128)S(1)}, u32[]{:S(2)}) copy-start(f32[7,16,16,128]{3,2,1,0:T(8,128)S(1)} %get-tuple-element.118) | copy-start | bytes 2752516
  92.2 5.5 %collective-permute-start.8 = (bf16[7,16,768]{2,1,0:T(8,128)(2,1)S(1)}, bf16[7,16,768]{2,1,0:T(8,128)(2,1)S(1)}, u32[]{:S(2)}, u32[]{:S(2)}) collective-permute-start(bf16[7,16,768]{2,1,0:T(8,128)(2,1)S(1)} %copy.55), channel_id=1, source_target_pairs={{16,0},{20,4},{24,8},{28,12},{0,16},{4,20},{8,24},{12,28},{17,1},{... | collective-permute-start | bytes 516104 | tf_op jit(solution)/shard_map/ppermute | solution.py:31
  119.3 2.9 %copy-start.3 = (bf16[6,7,16,128]{2,3,1,0:T(8,128)(2,1)S(1)}, bf16[6,7,16,128]{2,3,1,0:T(8,128)(2,1)}, u32[]{:S(2)}) copy-start(bf16[6,7,16,128]{2,3,1,0:T(8,128)(2,1)} %copy-done.2) | copy-start | bytes 516100 | tf_op jit(solution)/shard_map/while
  158.2 2.9 %copy-start.3 = (bf16[6,7,16,128]{2,3,1,0:T(8,128)(2,1)S(1)}, bf16[6,7,16,128]{2,3,1,0:T(8,128)(2,1)}, u32[]{:S(2)}) copy-start(bf16[6,7,16,128]{2,3,1,0:T(8,128)(2,1)} %copy-done.2) | copy-start | bytes 516100 | tf_op jit(solution)/shard_map/while
  184.2 2.9 %copy-start.3 = (bf16[6,7,16,128]{2,3,1,0:T(8,128)(2,1)S(1)}, bf16[6,7,16,128]{2,3,1,0:T(8,128)(2,1)}, u32[]{:S(2)}) copy-start(bf16[6,7,16,128]{2,3,1,0:T(8,128)(2,1)} %copy-done.2) | copy-start | bytes 516100 | tf_op jit(solution)/shard_map/while
  187.1 9.6 %copy-start.5 = (f32[1,16,16,128]{1,3,2,0:T(8,128)S(1)}, f32[1,16,16,128]{1,3,2,0:T(8,128)}, u32[]{:S(2)}) copy-start(f32[1,16,16,128]{1,3,2,0:T(8,128)} %copy.53) | copy-start | bytes 393220
  188.9 7.8 %collective-permute-start.9 = (f32[16,768]{0,1:T(8,128)S(1)}, f32[16,768]{0,1:T(8,128)S(1)}, u32[]{:S(2)}, u32[]{:S(2)}) collective-permute-start(f32[16,768]{0,1:T(8,128)S(1)} %select_bitcast_fusion), channel_id=1, source_target_pairs={{16,0},{20,4},{24,8},{28,12},{0,16},{4,20},{8,24},{12,28},{17,1},{... | collective-permute-start | bytes 147464 | tf_op jit(solution)/shard_map/ppermute | solution.py:31
  (17 other events, 22.0 us)
where the time goes:
time: 209 us; the launch traced here: 207 us
  local copies, waits for them, and re-layouts  68.6 us (33%)
  other arithmetic  59.2 us (28%)
  waiting for transfers between devices  24.5 us (12%)
  starting transfers between devices  18.5 us (9%)
  matrix products  18.5 us (9%)
  between operations  17 us (8%)
    another operation x12, local copies, waits for them, and re-layouts, absorb(): depth = jnp.cumsum(tau, axis=1)  18.4 us
    reduce_sum x6, other arithmetic, absorb(): return jnp.sum((jnp.exp(-above) - jnp.exp(-depth)) * band_weight, axis=-1)  16.8 us
    dot_general x6, matrix products, absorb(): jnp.dot(second, w_third, preferred_element_type=jnp.float32) + b_third  16.4 us
    ppermute x4, waiting for transfers between devices, extended(): lax.ppermute(head, axis, [((i + 1) % count, i) for i in range(ends)])  12.8 us
    mul x6, local copies, waits for them, and re-layouts, absorb(): 0.15 * jax.nn.softplus(jnp.dot(second, w_third, preferred_element_type=jn...  11.2 us
    ppermute x2, waiting for transfers between devices, shifted_2(): return lax.ppermute(block, axis, route)  9.7 us
    ppermute x4, starting transfers between devices, extended(): lax.ppermute(tail, axis, [(i, (i + 1) % count) for i in range(ends)])  9.28 us
    scatter-add x1, other arithmetic, body(): temper = now[2].reshape(now.shape[1], cells).at[:, listed].add(heat.T)  9.02 us
  transfers between devices with their start and end apart: 10, of which 4 were waited for; matrix products, arithmetic and copies ran while one was open for 9% of the time, Pallas kernels for 0%

commit v1 on v0

v1 whole, which is shorter than its diff:
```python
import functools
import math

import jax
import jax.numpy as jnp
from jax import lax
from jax.experimental import pallas as pl
from jax.experimental.pallas import tpu as pltpu
from jax.sharding import PartitionSpec as P

SMAX = 32
POLAR = 4
MESH = pl.DeviceIdType.MESH
LOG2E = math.log2(math.e)
RATE = 0.15


def column(row, lanes):
    return jnp.transpose(jnp.broadcast_to(row, (lanes, row.shape[1])))


def flipped(weight):
    rows = weight.shape[0]
    eye = (
        lax.broadcasted_iota(jnp.int32, (rows, rows), 0)
        == lax.broadcasted_iota(jnp.int32, (rows, rows), 1)
    ).astype(jnp.float32).astype(jnp.bfloat16)
    return lax.dot_general(
        weight, eye, (((0,), (0,)), ((), ())), preferred_element_type=jnp.float32
    )


def kernel(
    dims,
    prev_ref,
    now_ref,
    stride_ref,
    flen_ref,
    zcoef_ref,
    count_ref,
    mcoef_ref,
    fcoef_ref,
    w1_ref,
    b1_ref,
    w2_ref,
    b2_ref,
    w3_ref,
    b3_ref,
    band_ref,
    list_ref,
    prev_out,
    now_out,
    now0,
    now1,
    prev1,
    temper,
    feats,
    lon_out,
    lon_in,
    lat_in,
    w1big,
    w2t,
    w3t,
    bias1,
    bias2,
    bias3,
    start3,
    first,
    second,
    depth,
    heat,
    mask,
    send_sem,
    recv_sem,
):
    nvar, lev, rows, lanes, n_lon, n_lat = dims
    hid = w2_ref.shape[0]
    gpt = w3_ref.shape[1]
    lon = lax.axis_index("lon")
    lat = lax.axis_index("lat")
    east = lax.rem(lon + 1, n_lon)
    west = lax.rem(lon + n_lon - 1, n_lon)
    at_top = lat == 0
    at_end = lat == n_lat - 1
    polar = jnp.logical_or(at_top, at_end)
    pstart = jnp.where(at_top, 0, rows - POLAR)
    body_lo = jnp.where(at_top, POLAR, 0)
    body_hi = jnp.where(at_end, rows - POLAR, rows)

    barrier = pltpu.get_barrier_semaphore()
    for peer in (east, west):
        pl.semaphore_signal(barrier, inc=1, device_id={"lon": peer}, device_id_type=MESH)

    @pl.when(lat > 0)
    def _():
        pl.semaphore_signal(barrier, inc=1, device_id={"lat": lat - 1}, device_id_type=MESH)

    @pl.when(lat < n_lat - 1)
    def _():
        pl.semaphore_signal(barrier, inc=1, device_id={"lat": lat + 1}, device_id_type=MESH)

    lane = lax.broadcasted_iota(jnp.int32, (lev, lanes), 1)

    def zonal(turn, side, whole):
        part = pl.ds(0, nvar + 1) if whole else pl.ds(nvar, 1)
        return pltpu.make_async_remote_copy(
            src_ref=lon_out.at[turn, side, part],
            dst_ref=lon_in.at[turn, side, part],
            send_sem=send_sem.at[turn, side],
            recv_sem=recv_sem.at[turn, side],
            device_id={"lon": west if side == 0 else east},
            device_id_type=MESH,
        )

    def merid_copy(turn, side, src):
        return pltpu.make_async_remote_copy(
            src_ref=src.at[:, 1 if side == 0 else rows],
            dst_ref=lat_in.at[turn, side],
            send_sem=send_sem.at[turn, 2 + side],
            recv_sem=recv_sem.at[turn, 2 + side],
            device_id={"lat": lat - 1 if side == 0 else lat + 1},
            device_id_type=MESH,
        )

    def send_rows(turn, src):
        @pl.when(lat > 0)
        def _():
            merid_copy(turn, 0, src).start()

        @pl.when(lat < n_lat - 1)
        def _():
            merid_copy(turn, 1, src).start()

    def send_sides(turn, src):
        def gather_edges(j, edges):
            head, tail = edges
            for v in range(nvar):
                x = src[v, j + 1]
                place = v * rows + j
                head = jnp.where(lane == place, pltpu.roll(x, place, 1), head)
                tail = jnp.where(lane == place, pltpu.roll(x, lax.rem(place + 1, lanes), 1), tail)
            return head, tail

        zero = jnp.zeros((lev, lanes), jnp.float32)
        head, tail = lax.fori_loop(0, rows, gather_edges, (zero, zero))
        lon_out[turn, 0, nvar] = head
        lon_out[turn, 1, nvar] = tail

        @pl.when(polar)
        def _():
            for v in range(nvar):
                head = jnp.zeros((lev, lanes), jnp.float32)
                tail = head
                for q in range(POLAR):
                    x = src[v, pstart + q + 1]
                    here = lane // SMAX == q
                    head = jnp.where(here, pltpu.roll(x, (SMAX * q) % lanes, 1), head)
                    tail = jnp.where(here, pltpu.roll(x, (SMAX * q + SMAX) % lanes, 1), tail)
                lon_out[turn, 0, v] = head
                lon_out[turn, 1, v] = tail
            zonal(turn, 0, True).start()
            zonal(turn, 1, True).start()

        @pl.when(jnp.logical_not(polar))
        def _():
            zonal(turn, 0, False).start()
            zonal(turn, 1, False).start()

    def finish(turn, src):
        @pl.when(polar)
        def _():
            zonal(turn, 0, True).wait()
            zonal(turn, 1, True).wait()

        @pl.when(jnp.logical_not(polar))
        def _():
            zonal(turn, 0, False).wait()
            zonal(turn, 1, False).wait()

        @pl.when(lat > 0)
        def _():
            merid_copy(turn, 0, src).wait_send()
            merid_copy(turn, 1, src).wait_recv()
            for v in range(nvar):
                src[v, 0] = lat_in[turn, 1, v]

        @pl.when(lat < n_lat - 1)
        def _():
            merid_copy(turn, 1, src).wait_send()
            merid_copy(turn, 0, src).wait_recv()
            for v in range(nvar):
                src[v, rows + 1] = lat_in[turn, 0, v]

        zero = jnp.zeros((lev, lanes), jnp.float32)

        @pl.when(at_top)
        def _():
            for v in range(nvar):
                src[v, 0] = zero

        @pl.when(at_end)
        def _():
            for v in range(nvar):
                src[v, rows + 1] = zero

    def leap(turn, src, get_prev, put):
        mcoef = column(mcoef_ref[...], lanes)
        fcoef = column(fcoef_ref[...], lanes)
        from_east = lon_in.at[turn, 0]
        from_west = lon_in.at[turn, 1]

        def emit(v, j, x, diff, ends, zu, mv):
            tend = zu * diff - mv * (src[v, j + 2] - src[v, j])
            tend = tend + fcoef * (ends - 2.0 * x)
            old = get_prev(v, j)
            new = old + tend
            put(v, j, x + 0.1 * (old - 2.0 * x + new), new)

        def plain(j, carry):
            zu = -zcoef_ref[j] * src[0, j + 1]
            mv = mcoef * src[1, j + 1]
            pe = from_east[nvar]
            pw = from_west[nvar]
            for v in range(nvar):
                x = src[v, j + 1]
                place = v * rows + j
                plus = jnp.where(
                    lane == lanes - 1,
                    pltpu.roll(pe, lanes - 1 - place, 1),
                    pltpu.roll(x, lanes - 1, 1),
                )
                minus = jnp.where(
                    lane == 0, pltpu.roll(pw, lax.rem(lanes - place, lanes), 1), pltpu.roll(x, 1, 1)
                )
                emit(v, j, x, plus - minus, plus + minus, zu, mv)
            return carry

        lax.fori_loop(body_lo, body_hi, plain, 0)

        @pl.when(polar)
        def _():
            for q in range(POLAR):
                j = pstart + q
                s = stride_ref[j]
                m = flen_ref[j]
                inv = 1.0 / jnp.full((lev, lanes), s, jnp.int32).astype(jnp.float32)
                zu = (-zcoef_ref[j] * src[0, j + 1])
                mv = mcoef * src[1, j + 1]
                for v in range(nvar):
                    x = src[v, j + 1]
                    he = pltpu.roll(from_east[v], (lanes - SMAX * q) % lanes, 1)
                    hw = pltpu.roll(from_west[v], (lanes - SMAX - SMAX * q) % lanes, 1)
                    pair = []
                    for n in (s, m):
                        plus = pltpu.roll(jnp.where(lane < n, he, x), lanes - n, 1)
                        minus = pltpu.roll(jnp.where(lane >= lanes - n, hw, x), n, 1)
                        pair.append((plus, minus))
                    diff = (pair[0][0] - pair[0][1]) * inv
                    emit(v, j, x, diff, pair[1][0] + pair[1][1], zu, mv)

    def load(j, carry):
        for v in range(nvar):
            now0[v, j + 1] = now_ref[v, pl.ds(j, lev, stride=rows), :]
        return carry

    lax.fori_loop(0, rows, load, 0)
    pl.semaphore_wait(
        barrier, 2 + jnp.where(lat > 0, 1, 0) + jnp.where(lat < n_lat - 1, 1, 0)
    )

    send_rows(0, now0)
    send_sides(0, now0)

    expand = (
        lax.broadcasted_iota(jnp.int32, (nvar, nvar * lev), 1) // lev
        == lax.broadcasted_iota(jnp.int32, (nvar, nvar * lev), 0)
    ).astype(jnp.float32).astype(jnp.bfloat16)
    spread = lax.dot_general(
        w1_ref[...], expand, (((0,), (0,)), ((), ())), preferred_element_type=jnp.float32
    )
    level = lax.broadcasted_iota(jnp.int32, (hid, nvar * lev), 1) % lev
    for k in range(lev):
        w1big[pl.ds(k * hid, hid), :] = jnp.where(level == k, spread, 0.0).astype(jnp.bfloat16)
    w2t[...] = flipped(w2_ref[...]).astype(jnp.bfloat16)
    w3t[...] = flipped(w3_ref[...]).astype(jnp.bfloat16)
    bias1[...] = column(0.5 * b1_ref[...], 2 * lanes)
    bias2[...] = column(0.5 * b2_ref[...], 2 * lanes)
    bias3[...] = column(LOG2E * b3_ref[...], 2 * lanes)
    start3[...] = column(jnp.log2(band_ref[...]) * (-1.0 / RATE), 2 * lanes)
    listed = list_ref[...]
    slots = listed.shape[1]
    live = lax.broadcasted_iota(jnp.int32, (1, slots), 1) < count_ref[0, lon]
    row_hot = jnp.logical_and(
        lax.broadcasted_iota(jnp.int32, (rows, slots), 0) == listed // lanes, live
    ).astype(jnp.float32).astype(jnp.bfloat16)
    lane_hot = (
        lax.broadcasted_iota(jnp.int32, (lanes, slots), 0) == listed % lanes
    ).astype(jnp.float32).astype(jnp.bfloat16)
    mask[...] = lax.dot_general(
        row_hot, lane_hot, (((1,), (1,)), ((), ())), preferred_element_type=jnp.float32
    )

    finish(0, now0)

    def put_first(v, j, filtered, new):
        prev1[v, j] = filtered
        now1[v, j + 1] = new

    leap(0, now0, lambda v, j: prev_ref[v, pl.ds(j, lev, stride=rows), :], put_first)
    send_rows(1, now1)
    send_sides(1, now1)
    finish(1, now1)

    def put_second(v, j, filtered, new):
        prev_out[v, pl.ds(j, lev, stride=rows), :] = filtered
        feats[j, pl.ds(v * lev, lev), :] = new.astype(jnp.bfloat16)
        if v == 2:
            temper[j] = new
        else:
            now_out[v, pl.ds(j, lev, stride=rows), :] = new

    leap(1, now1, lambda v, j: prev1[v, j], put_second)

    wide = 2 * lanes
    chunk = 16

    def absorb(pair, carry):
        cells = jnp.concatenate([feats[2 * pair], feats[2 * pair + 1]], axis=1)
        for k in range(lev):
            part = pl.ds(k * hid, hid)
            half = 0.5 * jnp.dot(w1big[part, :], cells, preferred_element_type=jnp.float32) + bias1[...]
            first[part, :] = (half + half * jnp.tanh(half)).astype(jnp.bfloat16)
        for k in range(lev):
            part = pl.ds(k * hid, hid)
            half = 0.5 * jnp.dot(w2t[...], first[part, :], preferred_element_type=jnp.float32) + bias2[...]
            second[part, :] = (half + half * jnp.tanh(half)).astype(jnp.bfloat16)
        depth[...] = start3[...]
        top = jnp.zeros((8, wide), jnp.float32)
        for g in range(0, gpt, 8):
            top = top + jnp.exp2(-RATE * start3[pl.ds(g, 8), :])

        def one_level(k, above):
            part = pl.ds(pl.multiple_of(k * hid, hid), hid)
            raw = jnp.dot(w3t[...], second[part, :], preferred_element_type=jnp.float32)
            total = jnp.zeros((8, wide), jnp.float32)
            for g in range(0, gpt, chunk):
                at = pl.ds(g, chunk)
                y = raw[g : g + chunk] * LOG2E + bias3[at, :]
                soft = jnp.maximum(y, jnp.log2(1.0 + jnp.exp2(jnp.minimum(y, 64.0))))
                here = depth[at, :] + soft
                depth[at, :] = here
                left = jnp.exp2(-RATE * here)
                for piece in range(0, chunk, 8):
                    total = total + left[piece : piece + 8]
            heat[pl.ds(k, 1), :] = jnp.sum(above - total, axis=0, keepdims=True)
            return total

        lax.fori_loop(0, lev, one_level, top, unroll=4)
        for side in range(2):
            j = 2 * pair + side
            warm = heat[:, side * lanes : (side + 1) * lanes] * mask[pl.ds(j, 1), :]
            now_out[2, pl.ds(j, lev, stride=rows), :] = temper[j] + warm
        return carry

    lax.fori_loop(0, rows // 2, absorb, 0)


def body(
    state_prev,
    state_now,
    stride_table,
    filter_len,
    zonal_coef,
    merid_coef,
    filter_coef,
    w_first,
    b_first,
    w_second,
    b_second,
    w_third,
    b_third,
    band_weight,
    sunlit_cols,
    sunlit_count,
):
    nvar, lev, rows, lanes = state_now.shape
    dims = (nvar, lev, rows, lanes, lax.axis_size("lon"), lax.axis_size("lat"))
    hid = w_second.shape[0]
    gpt = w_third.shape[1]
    flat = (nvar, lev * rows, lanes)
    vmem = pl.BlockSpec(memory_space=pltpu.VMEM)
    smem = pl.BlockSpec(memory_space=pltpu.SMEM)
    f32, bf16 = jnp.float32, jnp.bfloat16
    tile = (lev, lanes)
    shape = jax.ShapeDtypeStruct(flat, f32)
    prev, now = pl.pallas_call(
        functools.partial(kernel, dims),
        out_shape=(shape, shape),
        in_specs=[vmem] * 2 + [smem] * 4 + [vmem] * 10,
        out_specs=(vmem, vmem),
        scratch_shapes=[
            pltpu.VMEM((nvar, rows + 2) + tile, f32),
            pltpu.VMEM((nvar, rows + 2) + tile, f32),
            pltpu.VMEM((nvar, rows) + tile, f32),
            pltpu.VMEM((rows,) + tile, f32),
            pltpu.VMEM((rows, nvar * lev, lanes), bf16),
            pltpu.VMEM((2, 2, nvar + 1) + tile, f32),
            pltpu.VMEM((2, 2, nvar + 1) + tile, f32),
            pltpu.VMEM((2, 2, nvar) + tile, f32),
            pltpu.VMEM((lev * hid, nvar * lev), bf16),
            pltpu.VMEM((hid, hid), bf16),
            pltpu.VMEM((gpt, hid), bf16),
            pltpu.VMEM((hid, 2 * lanes), f32),
            pltpu.VMEM((hid, 2 * lanes), f32),
            pltpu.VMEM((gpt, 2 * lanes), f32),
            pltpu.VMEM((gpt, 2 * lanes), f32),
            pltpu.VMEM((lev * hid, 2 * lanes), bf16),
            pltpu.VMEM((lev * hid, 2 * lanes), bf16),
            pltpu.VMEM((gpt, 2 * lanes), f32),
            pltpu.VMEM((lev, 2 * lanes), f32),
            pltpu.VMEM((rows, lanes), f32),
            pltpu.SemaphoreType.DMA((2, 4)),
            pltpu.SemaphoreType.DMA((2, 4)),
        ],
        compiler_params=pltpu.CompilerParams(
            collective_id=0, has_side_effects=True, vmem_limit_bytes=40 * 1024 * 1024
        ),
    )(
        state_prev.reshape(flat),
        state_now.reshape(flat),
        stride_table,
        filter_len,
        zonal_coef,
        sunlit_count,
        merid_coef[None],
        filter_coef[None],
        w_first,
        b_first[None],
        w_second,
        b_second[None],
        w_third,
        b_third[None],
        band_weight[None],
        sunlit_cols.reshape(1, -1),
    )
    return prev.reshape(state_prev.shape), now.reshape(state_now.shape)


def solution(mesh):
    field = P(None, None, "lat", "lon")
    in_specs = (
        (field, field, P("lat"), P("lat"), P("lat"))
        + (P(),) * 9
        + (P("lat", "lon", None), P("lat", None))
    )
    return jax.shard_map(
        body, mesh=mesh, in_specs=in_specs, out_specs=(field, field), check_vma=False
    )
```

time: 209 us -> 57.4 us (0.27)
  other arithmetic: 59.2 us -> 0 us
  local copies, waits for them, and re-layouts: 68.6 us -> 13 us
  Pallas kernels: 0 us -> 43.3 us
  waiting for transfers between devices: 24.5 us -> 0 us
  matrix products: 18.5 us -> 0 us
  starting transfers between devices: 18.5 us -> 0 us
  between operations: 17 us -> 0.68 us
    pallas_call x0 -> x1, Pallas kernels: none -> 43.3 us  [body(): pl.pallas_call(functools.partial(kernel, dims), out_shape=(shape, shape),...]
    ppermute x10 -> x0, waiting for transfers between devices: 24.5 us -> none  [the longest x4 12.8 us: extended(): lax.ppermute(head, axis, [((i + 1) % count, i) for i in range(ends)])]
    another operation x13 -> x0, local copies, waits for them, and re-layouts: 18.7 us -> none  [the longest x12 18.4 us: absorb(): depth = jnp.cumsum(tau, axis=1)]
    dot_general x12 -> x0, matrix products: 18.5 us -> none  [the longest x6 16.4 us: absorb(): jnp.dot(second, w_third, preferred_element_type=jnp.float32) + b_third]
    ppermute x10 -> x0, starting transfers between devices: 18.5 us -> none  [the longest x4 9.28 us: extended(): lax.ppermute(tail, axis, [(i, (i + 1) % count) for i in range(ends)])]
    reduce_sum x6 -> x0, other arithmetic: 16.8 us -> none  [absorb(): return jnp.sum((jnp.exp(-above) - jnp.exp(-depth)) * band_weight, axis=-1)]
    mul x6 -> x0, local copies, waits for them, and re-layouts: 11.2 us -> none  [absorb(): 0.15 * jax.nn.softplus(jnp.dot(second, w_third, preferred_element_type=jn...]
    gather x3 -> x0, local copies, waits for them, and re-layouts: 10.8 us -> none  [the longest x1 6.03 us: body(): feats_t = jnp.take(flat, listed, axis=2).astype(jnp.bfloat16)]
  transfers between devices with their start and end apart: 10 -> 0, of which waited for: 4 -> 0; matrix products, arithmetic and copies ran while one was open for 9% -> 0% of each run, Pallas kernels for 0% -> 0%
where the time goes in v1:
time: 57.4 us; the launch traced here: 56.9 us
  Pallas kernels  43.3 us (75%)
  local copies, waits for them, and re-layouts  13 us (23%)
  between operations  0.68 us (1%)
    pallas_call x1, Pallas kernels, body(): pl.pallas_call(functools.partial(kernel, dims), out_shape=(shape, shape),...  43.3 us
    unnamed x34, local copies, waits for them, and re-layouts  13 us

profile of v1, /device:TPU:0, one launch (start us, length us, event | category | flops | bytes accessed | tf_op | source)
XLA Modules:
  0.0 56.9 jit_solution(4533105201069850113)
XLA Ops:
  0.6 0.0 copy-start.3
  0.6 0.0 copy-start.6
  0.7 0.7 %copy-done.3 = bf16[64,64]{1,0:T(8,128)(2,1)S(1)} copy-done((bf16[64,64]{1,0:T(8,128)(2,1)S(1)}, bf16[64,64]{1,0:T(8,128)(2,1)}, u32[]{:S(2)}) %copy-start.3) | copy-done | bytes 8216
  1.4 0.0 copy-done.6
  1.4 0.0 copy-start
  1.4 1.2 %copy-done = f32[7,16,16,128]{3,2,1,0:T(8,128)S(1)} copy-done((f32[7,16,16,128]{3,2,1,0:T(8,128)S(1)}, f32[7,16,16,128]{3,2,1,0:T(8,128)}, u32[]{:S(2)}) %copy-start) | copy-done | bytes 917528
  2.5 0.0 copy-start.1
  2.5 1.2 %copy-done.1 = f32[7,16,16,128]{3,2,1,0:T(8,128)S(1)} copy-done((f32[7,16,16,128]{3,2,1,0:T(8,128)S(1)}, f32[7,16,16,128]{3,2,1,0:T(8,128)}, u32[]{:S(2)}) %copy-start.1) | copy-done | bytes 917528
  3.7 0.0 copy-start.2
  3.7 0.8 %copy-done.2 = bf16[64,224]{1,0:T(8,128)(2,1)S(1)} copy-done((bf16[64,224]{1,0:T(8,128)(2,1)S(1)}, bf16[64,224]{1,0:T(8,128)(2,1)}, u32[]{:S(2)}) %copy-start.2) | copy-done | bytes 28696
  4.5 0.7 %copy-done.4 = s32[1,1,1536]{2,1,0:T(1,128)S(1)} copy-done((s32[1,1,1536]{2,1,0:T(1,128)S(1)}, s32[1,1,1536]{2,1,0:T(1,128)}, u32[]{:S(2)}) %copy-start.4) | copy-done | bytes 6168
  5.2 0.7 %copy-done.5 = bf16[7,64]{1,0:T(8,128)(2,1)S(1)} copy-done((bf16[7,64]{1,0:T(8,128)(2,1)S(1)}, bf16[7,64]{1,0:T(8,128)(2,1)}, u32[]{:S(2)}) %copy-start.5) | copy-done | bytes 920
  5.9 0.7 %copy-done.7 = f32[224]{0:T(256)S(1)} copy-done((f32[224]{0:T(256)S(1)}, f32[224]{0:T(256)}, u32[]{:S(2)}) %copy-start.7) | copy-done | bytes 920
  6.5 0.7 %copy-done.8 = s32[16]{0:T(128)S(1)} copy-done((s32[16]{0:T(128)S(1)}, s32[16]{0:T(128)}, u32[]{:S(2)}) %copy-start.8) | copy-done | bytes 88
  7.2 0.7 %copy-done.9 = s32[16]{0:T(128)S(1)} copy-done((s32[16]{0:T(128)S(1)}, s32[16]{0:T(128)}, u32[]{:S(2)}) %copy-start.9) | copy-done | bytes 88
  7.8 0.7 %copy-done.10 = f32[16]{0:T(128)S(1)} copy-done((f32[16]{0:T(128)S(1)}, f32[16]{0:T(128)}, u32[]{:S(2)}) %copy-start.10) | copy-done | bytes 88
  8.5 0.7 %copy-done.11 = s32[1,8]{1,0:T(1,128)S(1)} copy-done((s32[1,8]{1,0:T(1,128)S(1)}, s32[1,8]{1,0:T(1,128)}, u32[]{:S(2)}) %copy-start.11) | copy-done | bytes 56
  9.2 0.7 %copy-done.12 = f32[16]{0:T(128)S(1)} copy-done((f32[16]{0:T(128)S(1)}, f32[16]{0:T(128)}, u32[]{:S(2)}) %copy-start.12) | copy-done | bytes 88
  9.8 0.7 %copy-done.13 = f32[16]{0:T(128)S(1)} copy-done((f32[16]{0:T(128)S(1)}, f32[16]{0:T(128)}, u32[]{:S(2)}) %copy-start.13) | copy-done | bytes 88
  10.5 0.7 %copy-done.14 = f32[64]{0:T(128)S(1)} copy-done((f32[64]{0:T(128)S(1)}, f32[64]{0:T(128)}, u32[]{:S(2)}) %copy-start.14) | copy-done | bytes 280
  11.1 0.7 %copy-done.15 = f32[64]{0:T(128)S(1)} copy-done((f32[64]{0:T(128)S(1)}, f32[64]{0:T(128)}, u32[]{:S(2)}) %copy-start.15) | copy-done | bytes 280
  11.8 43.3 %shard_map.167 = (f32[7,256,128]{2,1,0:T(8,128)S(1)}, f32[7,256,128]{2,1,0:T(8,128)S(1)}) custom-call(f32[7,256,128]{2,1,0:T(8,128)S(1)} %bitcast.11, f32[7,256,128]{2,1,0:T(8,128)S(1)} %bitcast.12, s32[16]{0:T(128)S(1)} %copy-done.8, s32[16]{0:T(128)S(1)} %copy-done.9, f32[16]{0:T(128)S(1)} %copy-done.10, s32[1,8]{1,0:T(1,128)S(1)} %copy-done.11, ...), custom_call_target="tpu_custom_call" | custom-call | tf_op jit(solution)/shard_map/pallas_call | solution.py:396
  55.1 0.9 %copy.20 = f32[7,16,16,128]{3,2,1,0:T(8,128)} copy(f32[7,16,16,128]{3,2,1,0:T(8,128)S(1)} %bitcast.14) | data formatting | bytes 1835008
  56.0 0.9 %copy.21 = f32[7,16,16,128]{3,2,1,0:T(8,128)} copy(f32[7,16,16,128]{3,2,1,0:T(8,128)S(1)} %bitcast.13) | data formatting | bytes 1835008
  (11 shorter events, 0.0 us)
Async XLA Ops:
  0.6 0.7 %copy-start.3 = (bf16[64,64]{1,0:T(8,128)(2,1)S(1)}, bf16[64,64]{1,0:T(8,128)(2,1)}, u32[]{:S(2)}) copy-start(bf16[64,64]{1,0:T(8,128)(2,1)} %w2_ref.1) | copy-start | bytes 24580
  0.6 0.7 %copy-start.6 = (f32[224]{0:T(256)S(1)}, f32[224]{0:T(256)}, u32[]{:S(2)}) copy-start(f32[224]{0:T(256)} %param.28) | copy-start | bytes 2692
  1.4 1.2 %copy-start = (f32[7,16,16,128]{3,2,1,0:T(8,128)S(1)}, f32[7,16,16,128]{3,2,1,0:T(8,128)}, u32[]{:S(2)}) copy-start(f32[7,16,16,128]{3,2,1,0:T(8,128)} %param.16) | copy-start | bytes 2752516
  2.5 1.2 %copy-start.1 = (f32[7,16,16,128]{3,2,1,0:T(8,128)S(1)}, f32[7,16,16,128]{3,2,1,0:T(8,128)}, u32[]{:S(2)}) copy-start(f32[7,16,16,128]{3,2,1,0:T(8,128)} %param.17) | copy-start | bytes 2752516
  3.7 0.8 %copy-start.2 = (bf16[64,224]{1,0:T(8,128)(2,1)S(1)}, bf16[64,224]{1,0:T(8,128)(2,1)}, u32[]{:S(2)}) copy-start(bf16[64,224]{1,0:T(8,128)(2,1)} %w3_ref.1) | copy-start | bytes 86020
  4.5 0.7 %copy-start.4 = (s32[1,1,1536]{2,1,0:T(1,128)S(1)}, s32[1,1,1536]{2,1,0:T(1,128)}, u32[]{:S(2)}) copy-start(s32[1,1,1536]{2,1,0:T(1,128)} %param.30) | copy-start | bytes 18436
  5.2 0.7 %copy-start.5 = (bf16[7,64]{1,0:T(8,128)(2,1)S(1)}, bf16[7,64]{1,0:T(8,128)(2,1)}, u32[]{:S(2)}) copy-start(bf16[7,64]{1,0:T(8,128)(2,1)} %w1_ref.1) | copy-start | bytes 2692
  5.8 0.7 %copy-start.7 = (f32[224]{0:T(256)S(1)}, f32[224]{0:T(256)}, u32[]{:S(2)}) copy-start(f32[224]{0:T(256)} %param.29) | copy-start | bytes 2692
  6.5 0.7 %copy-start.8 = (s32[16]{0:T(128)S(1)}, s32[16]{0:T(128)}, u32[]{:S(2)}) copy-start(s32[16]{0:T(128)} %stride_ref.1) | copy-start | bytes 196
  7.2 0.7 %copy-start.9 = (s32[16]{0:T(128)S(1)}, s32[16]{0:T(128)}, u32[]{:S(2)}) copy-start(s32[16]{0:T(128)} %flen_ref.1) | copy-start | bytes 196
  7.8 0.7 %copy-start.10 = (f32[16]{0:T(128)S(1)}, f32[16]{0:T(128)}, u32[]{:S(2)}) copy-start(f32[16]{0:T(128)} %zcoef_ref.1) | copy-start | bytes 196
  8.5 0.7 %copy-start.11 = (s32[1,8]{1,0:T(1,128)S(1)}, s32[1,8]{1,0:T(1,128)}, u32[]{:S(2)}) copy-start(s32[1,8]{1,0:T(1,128)} %count_ref.1) | copy-start | bytes 100
  9.2 0.7 %copy-start.12 = (f32[16]{0:T(128)S(1)}, f32[16]{0:T(128)}, u32[]{:S(2)}) copy-start(f32[16]{0:T(128)} %param.21) | copy-start | bytes 196
  9.8 0.7 %copy-start.13 = (f32[16]{0:T(128)S(1)}, f32[16]{0:T(128)}, u32[]{:S(2)}) copy-start(f32[16]{0:T(128)} %param.22) | copy-start | bytes 196
  10.5 0.7 %copy-start.14 = (f32[64]{0:T(128)S(1)}, f32[64]{0:T(128)}, u32[]{:S(2)}) copy-start(f32[64]{0:T(128)} %param.24) | copy-start | bytes 772
  11.1 0.7 %copy-start.15 = (f32[64]{0:T(128)S(1)}, f32[64]{0:T(128)}, u32[]{:S(2)}) copy-start(f32[64]{0:T(128)} %param.26) | copy-start | bytes 772

commit v2 on v1

--- a/solution.py
+++ b/solution.py
@@ -30,49 +30,60 @@
     )
 
 
-def kernel(
-    dims,
-    prev_ref,
-    now_ref,
-    stride_ref,
-    flen_ref,
-    zcoef_ref,
-    count_ref,
-    mcoef_ref,
-    fcoef_ref,
-    w1_ref,
-    b1_ref,
-    w2_ref,
-    b2_ref,
-    w3_ref,
-    b3_ref,
-    band_ref,
-    list_ref,
-    prev_out,
-    now_out,
-    now0,
-    now1,
-    prev1,
-    temper,
-    feats,
-    lon_out,
-    lon_in,
-    lat_in,
-    w1big,
-    w2t,
-    w3t,
-    bias1,
-    bias2,
-    bias3,
-    start3,
-    first,
-    second,
-    depth,
-    heat,
-    mask,
-    send_sem,
-    recv_sem,
-):
+def kernel(dims, n_in, *refs):
+    operands, refs = refs[:n_in], refs[n_in:]
+    prev_out, now_out, refs = refs[0], refs[1], refs[2:]
+    held, refs = refs[:n_in], refs[n_in:]
+    (
+        prev_ref,
+        now_ref,
+        stride_ref,
+        flen_ref,
+        zcoef_ref,
+        count_ref,
+        mcoef_ref,
+        fcoef_ref,
+        w1_ref,
+        b1_ref,
+        w2_ref,
+        b2_ref,
+        w3_ref,
+        b3_ref,
+        band_ref,
+        list_ref,
+    ) = held
+    (
+        now0,
+        now1,
+        prev1,
+        temper,
+        feats,
+        lon_out,
+        lon_in,
+        lat_in,
+        w1big,
+        w2t,
+        w3t,
+        bias1,
+        bias2,
+        bias3,
+        start3,
+        first,
+        second,
+        depth,
+        heat,
+        hot,
+        own,
+        gone,
+        come,
+        heat_in,
+        grid,
+        load_sem,
+        send_sem,
+        recv_sem,
+        far_send,
+        far_recv,
+    ) = refs
     nvar, lev, rows, lanes, n_lon, n_lat = dims
     hid = w2_ref.shape[0]
     gpt = w3_ref.shape[1]
@@ -80,6 +91,7 @@
     lat = lax.axis_index("lat")
     east = lax.rem(lon + 1, n_lon)
     west = lax.rem(lon + n_lon - 1, n_lon)
+    far = lax.rem(lon + n_lon // 2, n_lon)
     at_top = lat == 0
     at_end = lat == n_lat - 1
     polar = jnp.logical_or(at_top, at_end)
@@ -87,8 +99,15 @@
     body_lo = jnp.where(at_top, POLAR, 0)
     body_hi = jnp.where(at_end, rows - POLAR, rows)
 
+    loads = [
+        pltpu.make_async_copy(src, dst, load_sem.at[i])
+        for i, (src, dst) in enumerate(zip(operands, held))
+    ]
+    for i in (1, *range(2, n_in), 0):
+        loads[i].start()
+
     barrier = pltpu.get_barrier_semaphore()
-    for peer in (east, west):
+    for peer in (east, west, far):
         pl.semaphore_signal(barrier, inc=1, device_id={"lon": peer}, device_id_type=MESH)
 
     @pl.when(lat > 0)
@@ -263,13 +282,17 @@
             now0[v, j + 1] = now_ref[v, pl.ds(j, lev, stride=rows), :]
         return carry
 
+    loads[1].wait()
     lax.fori_loop(0, rows, load, 0)
     pl.semaphore_wait(
-        barrier, 2 + jnp.where(lat > 0, 1, 0) + jnp.where(lat < n_lat - 1, 1, 0)
+        barrier, 3 + jnp.where(lat > 0, 1, 0) + jnp.where(lat < n_lat - 1, 1, 0)
     )
 
     send_rows(0, now0)
     send_sides(0, now0)
+
+    for i in (*range(2, n_in), 0):
+        loads[i].wait()
 
     expand = (
         lax.broadcasted_iota(jnp.int32, (nvar, nvar * lev), 1) // lev
@@ -287,18 +310,26 @@
     bias2[...] = column(0.5 * b2_ref[...], 2 * lanes)
     bias3[...] = column(LOG2E * b3_ref[...], 2 * lanes)
     start3[...] = column(jnp.log2(band_ref[...]) * (-1.0 / RATE), 2 * lanes)
-    listed = list_ref[...]
-    slots = listed.shape[1]
-    live = lax.broadcasted_iota(jnp.int32, (1, slots), 1) < count_ref[0, lon]
-    row_hot = jnp.logical_and(
-        lax.broadcasted_iota(jnp.int32, (rows, slots), 0) == listed // lanes, live
-    ).astype(jnp.float32).astype(jnp.bfloat16)
-    lane_hot = (
-        lax.broadcasted_iota(jnp.int32, (lanes, slots), 0) == listed % lanes
-    ).astype(jnp.float32).astype(jnp.bfloat16)
-    mask[...] = lax.dot_general(
-        row_hot, lane_hot, (((1,), (1,)), ((), ())), preferred_element_type=jnp.float32
-    )
+    half = list_ref.shape[1] // 2
+    mine = count_ref[0, lon]
+    other = count_ref[0, far]
+    slot = lax.broadcasted_iota(jnp.int32, (8, half), 1)
+    shift = jnp.minimum(other, half - 1)
+    moved = pltpu.roll(jnp.broadcast_to(list_ref[:, half:], (8, half)), shift, 1)
+    for side, (cols, live) in enumerate(
+        (
+            (jnp.broadcast_to(list_ref[:, :half], (8, half)), slot < mine),
+            (moved, jnp.logical_and(slot >= other, slot < other + mine - half)),
+        )
+    ):
+        cols = jnp.where(live, cols, -1)[:1]
+        at = pl.ds(side * half, half)
+        lane_hot = (
+            lax.broadcasted_iota(jnp.int32, (lanes, half), 0) == cols % lanes
+        ).astype(jnp.float32).astype(jnp.bfloat16)
+        for j in range(rows):
+            row_hot = (cols // lanes == j).astype(jnp.float32).astype(jnp.bfloat16)
+            hot[pl.ds(j * lanes, lanes), at] = lane_hot * row_hot
 
     finish(0, now0)
 
@@ -313,7 +344,8 @@
 
     def put_second(v, j, filtered, new):
         prev_out[v, pl.ds(j, lev, stride=rows), :] = filtered
-        feats[j, pl.ds(v * lev, lev), :] = new.astype(jnp.bfloat16)
+        at = pl.ds(pl.multiple_of(j * lanes, lanes), lanes)
+        feats[pl.ds(v * lev, lev), at] = new.astype(jnp.bfloat16)
         if v == 2:
             temper[j] = new
         else:
@@ -323,17 +355,49 @@
 
     wide = 2 * lanes
     chunk = 16
-
-    def absorb(pair, carry):
-        cells = jnp.concatenate([feats[2 * pair], feats[2 * pair + 1]], axis=1)
+    blocks = half // wide
+
+    def picked(at):
+        got = jnp.dot(feats[...], hot[:, pl.ds(at, wide)], preferred_element_type=jnp.float32)
+        return got.astype(jnp.bfloat16)
+
+    def to_far(b):
+        return pltpu.make_async_remote_copy(
+            src_ref=gone.at[b],
+            dst_ref=come.at[b],
+            send_sem=far_send.at[0, b],
+            recv_sem=far_recv.at[0, b],
+            device_id={"lon": far},
+            device_id_type=MESH,
+        )
+
+    def back(b):
+        return pltpu.make_async_remote_copy(
+            src_ref=heat.at[b],
+            dst_ref=heat_in.at[b],
+            send_sem=far_send.at[1, b],
+            recv_sem=far_recv.at[1, b],
+            device_id={"lon": far},
+            device_id_type=MESH,
+        )
+
+    for b in range(blocks):
+        gone[b] = picked(half + b * wide)
+        to_far(b).start()
+    for b in range(blocks):
+        own[b] = picked(b * wide)
+
+    def absorb(b, carry):
+        to_far(b).wait()
+        cells = own[b] + come[b]
         for k in range(lev):
             part = pl.ds(k * hid, hid)
-            half = 0.5 * jnp.dot(w1big[part, :], cells, preferred_element_type=jnp.float32) + bias1[...]
-            first[part, :] = (half + half * jnp.tanh(half)).astype(jnp.bfloat16)
+            x = 0.5 * jnp.dot(w1big[part, :], cells, preferred_element_type=jnp.float32) + bias1[...]
+            first[part, :] = (x + x * jnp.tanh(x)).astype(jnp.bfloat16)
         for k in range(lev):
             part = pl.ds(k * hid, hid)
-            half = 0.5 * jnp.dot(w2t[...], first[part, :], preferred_element_type=jnp.float32) + bias2[...]
-            second[part, :] = (half + half * jnp.tanh(half)).astype(jnp.bfloat16)
+            x = 0.5 * jnp.dot(w2t[...], first[part, :], preferred_element_type=jnp.float32) + bias2[...]
+            second[part, :] = (x + x * jnp.tanh(x)).astype(jnp.bfloat16)
         depth[...] = start3[...]
         top = jnp.zeros((8, wide), jnp.float32)
         for g in range(0, gpt, 8):
@@ -352,17 +416,35 @@
                 left = jnp.exp2(-RATE * here)
                 for piece in range(0, chunk, 8):
                     total = total + left[piece : piece + 8]
-            heat[pl.ds(k, 1), :] = jnp.sum(above - total, axis=0, keepdims=True)
+            heat[b, pl.ds(k, 1), :] = jnp.sum(above - total, axis=0, keepdims=True)
             return total
 
         lax.fori_loop(0, lev, one_level, top, unroll=4)
-        for side in range(2):
-            j = 2 * pair + side
-            warm = heat[:, side * lanes : (side + 1) * lanes] * mask[pl.ds(j, 1), :]
-            now_out[2, pl.ds(j, lev, stride=rows), :] = temper[j] + warm
+        back(b).start()
         return carry
 
-    lax.fori_loop(0, rows // 2, absorb, 0)
+    lax.fori_loop(0, blocks, absorb, 0)
+
+    def placed(warm, at):
+        high = warm.astype(jnp.bfloat16)
+        rest = warm - high.astype(jnp.float32)
+        mid = rest.astype(jnp.bfloat16)
+        low = (rest - mid.astype(jnp.float32)).astype(jnp.bfloat16)
+        out = lax.dot_general(
+            jnp.concatenate([high, mid, low], axis=0),
+            hot[:, pl.ds(at, half)],
+            (((1,), (1,)), ((), ())),
+            preferred_element_type=jnp.float32,
+        )
+        return out[:lev] + out[lev : 2 * lev] + out[2 * lev :]
+
+    grid[...] = placed(jnp.concatenate([heat[b] for b in range(blocks)], axis=1), 0)
+    for b in range(blocks):
+        back(b).wait()
+    grid[...] += placed(jnp.concatenate([heat_in[b] for b in range(blocks)], axis=1), half)
+    for j in range(rows):
+        warm = grid[:, j * lanes : (j + 1) * lanes]
+        now_out[2, pl.ds(j, lev, stride=rows), :] = temper[j] + warm
 
 
 def body(
@@ -388,44 +470,14 @@
     hid = w_second.shape[0]
     gpt = w_third.shape[1]
     flat = (nvar, lev * rows, lanes)
+    half = sunlit_cols.size // 2
+    wide = 2 * lanes
+    blocks = half // wide
     vmem = pl.BlockSpec(memory_space=pltpu.VMEM)
-    smem = pl.BlockSpec(memory_space=pltpu.SMEM)
     f32, bf16 = jnp.float32, jnp.bfloat16
     tile = (lev, lanes)
     shape = jax.ShapeDtypeStruct(flat, f32)
-    prev, now = pl.pallas_call(
-        functools.partial(kernel, dims),
-        out_shape=(shape, shape),
-        in_specs=[vmem] * 2 + [smem] * 4 + [vmem] * 10,
-        out_specs=(vmem, vmem),
-        scratch_shapes=[
-            pltpu.VMEM((nvar, rows + 2) + tile, f32),
-            pltpu.VMEM((nvar, rows + 2) + tile, f32),
-            pltpu.VMEM((nvar, rows) + tile, f32),
-            pltpu.VMEM((rows,) + tile, f32),
-            pltpu.VMEM((rows, nvar * lev, lanes), bf16),
-            pltpu.VMEM((2, 2, nvar + 1) + tile, f32),
-            pltpu.VMEM((2, 2, nvar + 1) + tile, f32),
-            pltpu.VMEM((2, 2, nvar) + tile, f32),
-            pltpu.VMEM((lev * hid, nvar * lev), bf16),
-            pltpu.VMEM((hid, hid), bf16),
-            pltpu.VMEM((gpt, hid), bf16),
-            pltpu.VMEM((hid, 2 * lanes), f32),
-            pltpu.VMEM((hid, 2 * lanes), f32),
-            pltpu.VMEM((gpt, 2 * lanes), f32),
-            pltpu.VMEM((gpt, 2 * lanes), f32),
-            pltpu.VMEM((lev * hid, 2 * lanes), bf16),
-            pltpu.VMEM((lev * hid, 2 * lanes), bf16),
-            pltpu.VMEM((gpt, 2 * lanes), f32),
-            pltpu.VMEM((lev, 2 * lanes), f32),
-            pltpu.VMEM((rows, lanes), f32),
-            pltpu.SemaphoreType.DMA((2, 4)),
-            pltpu.SemaphoreType.DMA((2, 4)),
-        ],
-        compiler_params=pltpu.CompilerParams(
-            collective_id=0, has_side_effects=True, vmem_limit_bytes=40 * 1024 * 1024
-        ),
-    )(
+    operands = (
         state_prev.reshape(flat),
         state_now.reshape(flat),
         stride_table,
@@ -443,6 +495,49 @@
         band_weight[None],
         sunlit_cols.reshape(1, -1),
     )
+    spaces = [pltpu.VMEM] * 2 + [pltpu.SMEM] * 4 + [pltpu.VMEM] * 10
+    prev, now = pl.pallas_call(
+        functools.partial(kernel, dims, len(operands)),
+        out_shape=(shape, shape),
+        in_specs=[pl.BlockSpec(memory_space=pltpu.HBM)] * len(operands),
+        out_specs=(vmem, vmem),
+        scratch_shapes=[space(x.shape, x.dtype) for space, x in zip(spaces, operands)]
+        + [
+            pltpu.VMEM((nvar, rows + 2) + tile, f32),
+            pltpu.VMEM((nvar, rows + 2) + tile, f32),
+            pltpu.VMEM((nvar, rows) + tile, f32),
+            pltpu.VMEM((rows,) + tile, f32),
+            pltpu.VMEM((nvar * lev, rows * lanes), bf16),
+            pltpu.VMEM((2, 2, nvar + 1) + tile, f32),
+            pltpu.VMEM((2, 2, nvar + 1) + tile, f32),
+            pltpu.VMEM((2, 2, nvar) + tile, f32),
+            pltpu.VMEM((lev * hid, nvar * lev), bf16),
+            pltpu.VMEM((hid, hid), bf16),
+            pltpu.VMEM((gpt, hid), bf16),
+            pltpu.VMEM((hid, wide), f32),
+            pltpu.VMEM((hid, wide), f32),
+            pltpu.VMEM((gpt, wide), f32),
+            pltpu.VMEM((gpt, wide), f32),
+            pltpu.VMEM((lev * hid, wide), bf16),
+            pltpu.VMEM((lev * hid, wide), bf16),
+            pltpu.VMEM((gpt, wide), f32),
+            pltpu.VMEM((blocks, lev, wide), f32),
+            pltpu.VMEM((rows * lanes, 2 * half), bf16),
+            pltpu.VMEM((blocks, nvar * lev, wide), bf16),
+            pltpu.VMEM((blocks, nvar * lev, wide), bf16),
+            pltpu.VMEM((blocks, nvar * lev, wide), bf16),
+            pltpu.VMEM((blocks, lev, wide), f32),
+            pltpu.VMEM((lev, rows * lanes), f32),
+            pltpu.SemaphoreType.DMA((len(operands),)),
+            pltpu.SemaphoreType.DMA((2, 4)),
+            pltpu.SemaphoreType.DMA((2, 4)),
+            pltpu.SemaphoreType.DMA((2, blocks)),
+            pltpu.SemaphoreType.DMA((2, blocks)),
+        ],
+        compiler_params=pltpu.CompilerParams(
+            collective_id=0, has_side_effects=True, vmem_limit_bytes=63 * 1024 * 1024
+        ),
+    )(*operands)
     return prev.reshape(state_prev.shape), now.reshape(state_now.shape)
 
 

time: 57.4 us -> 41.5 us (0.72)
  local copies, waits for them, and re-layouts: 13 us -> 3.19 us
  Pallas kernels: 43.3 us -> 37.5 us
    unnamed x34 -> x4, local copies, waits for them, and re-layouts: 13 us -> 3.19 us
    pallas_call x1, Pallas kernels: 43.3 us -> 37.5 us  [body(): pl.pallas_call(functools.partial(kernel, dims, len(operands)), out_shape=...]
where the time goes in v2:
time: 41.5 us; the launch traced here: 41.4 us
  Pallas kernels  37.5 us (90%)
  local copies, waits for them, and re-layouts  3.19 us (8%)
  between operations  0.65 us (2%)
    pallas_call x1, Pallas kernels, body(): pl.pallas_call(functools.partial(kernel, dims, len(operands)), out_shape=...  37.5 us
    unnamed x4, local copies, waits for them, and re-layouts  3.19 us

profile of v2, /device:TPU:0, one launch (start us, length us, event | category | flops | bytes accessed | tf_op | source)
XLA Modules:
  0.0 41.4 jit_solution(2898638345285677544)
XLA Ops:
  0.6 37.5 %shard_map.167 = (f32[7,256,128]{2,1,0:T(8,128)}, f32[7,256,128]{2,1,0:T(8,128)}) custom-call(f32[7,256,128]{2,1,0:T(8,128)} %bitcast.11, f32[7,256,128]{2,1,0:T(8,128)} %bitcast.12, s32[16]{0:T(128)} %refs_2_.1, s32[16]{0:T(128)} %refs_3_.1, f32[16]{0:T(128)} %refs_4_.1, s32[1,8]{1,0:T(1,128)} %refs_5_.1, f32[1,16]{1,0:T(1,128)} %bitcast.18, ...), custom_call_target="tpu_custom_call" | custom-call | tf_op jit(solution)/shard_map/pallas_call | solution.py:499
  38.2 0.0 copy-start
  38.2 2.3 %copy.20 = f32[7,16,16,128]{3,2,1,0:T(8,128)} copy(f32[7,16,16,128]{3,2,1,0:T(8,128)} %bitcast.14) | data formatting | bytes 1835008
  40.4 0.0 copy-done
  40.5 0.9 %copy.21 = f32[7,16,16,128]{3,2,1,0:T(8,128)} copy(f32[7,16,16,128]{3,2,1,0:T(8,128)S(1)} %bitcast.13) | data formatting | bytes 1835008
Async XLA Ops:
  38.2 2.3 %copy-start = (f32[7,256,128]{2,1,0:T(8,128)S(1)}, f32[7,256,128]{2,1,0:T(8,128)}, u32[]{:S(2)}) copy-start(f32[7,256,128]{2,1,0:T(8,128)} %get-tuple-element.5) | copy-start | bytes 2752516

commit v3 on v2

--- a/solution.py
+++ b/solution.py
@@ -32,7 +32,7 @@
 
 def kernel(dims, n_in, *refs):
     operands, refs = refs[:n_in], refs[n_in:]
-    prev_out, now_out, refs = refs[0], refs[1], refs[2:]
+    prev_hbm, now_hbm, refs = refs[0], refs[1], refs[2:]
     held, refs = refs[:n_in], refs[n_in:]
     (
         prev_ref,
@@ -53,6 +53,8 @@
         list_ref,
     ) = held
     (
+        prev_out,
+        now_out,
         now0,
         now1,
         prev1,
@@ -79,6 +81,7 @@
         heat_in,
         grid,
         load_sem,
+        save_sem,
         send_sem,
         recv_sem,
         far_send,
@@ -96,8 +99,10 @@
     at_end = lat == n_lat - 1
     polar = jnp.logical_or(at_top, at_end)
     pstart = jnp.where(at_top, 0, rows - POLAR)
-    body_lo = jnp.where(at_top, POLAR, 0)
-    body_hi = jnp.where(at_end, rows - POLAR, rows)
+    body_lo = jnp.where(at_top, 1, 0)
+    body_hi = jnp.where(at_end, rows // POLAR - 1, rows // POLAR)
+    per = lanes // 2 // rows
+    tiles = -(-nvar // per)
 
     loads = [
         pltpu.make_async_copy(src, dst, load_sem.at[i])
@@ -121,7 +126,7 @@
     lane = lax.broadcasted_iota(jnp.int32, (lev, lanes), 1)
 
     def zonal(turn, side, whole):
-        part = pl.ds(0, nvar + 1) if whole else pl.ds(nvar, 1)
+        part = pl.ds(0, nvar + tiles) if whole else pl.ds(nvar, tiles)
         return pltpu.make_async_remote_copy(
             src_ref=lon_out.at[turn, side, part],
             dst_ref=lon_in.at[turn, side, part],
@@ -150,20 +155,19 @@
         def _():
             merid_copy(turn, 1, src).start()
 
-    def send_sides(turn, src):
-        def gather_edges(j, edges):
-            head, tail = edges
-            for v in range(nvar):
-                x = src[v, j + 1]
-                place = v * rows + j
-                head = jnp.where(lane == place, pltpu.roll(x, place, 1), head)
-                tail = jnp.where(lane == place, pltpu.roll(x, lax.rem(place + 1, lanes), 1), tail)
-            return head, tail
-
-        zero = jnp.zeros((lev, lanes), jnp.float32)
-        head, tail = lax.fori_loop(0, rows, gather_edges, (zero, zero))
-        lon_out[turn, 0, nvar] = head
-        lon_out[turn, 1, nvar] = tail
+    def packed(edges, v, j, x):
+        t, place = v // per, (v % per) * rows + j
+        turned = pltpu.roll(x, lax.rem(2 * place + 1, lanes), 1)
+        edges = list(edges)
+        edges[t] = jnp.where(lane // 2 == place, turned, edges[t])
+        return tuple(edges)
+
+    no_edges = (jnp.zeros((lev, lanes), jnp.float32),) * tiles
+
+    def send_sides(turn, src, edges):
+        for t in range(tiles):
+            lon_out[turn, 0, nvar + t] = edges[t]
+            lon_out[turn, 1, nvar + t] = edges[t]
 
         @pl.when(polar)
         def _():
@@ -172,9 +176,9 @@
                 tail = head
                 for q in range(POLAR):
                     x = src[v, pstart + q + 1]
-                    here = lane // SMAX == q
-                    head = jnp.where(here, pltpu.roll(x, (SMAX * q) % lanes, 1), head)
-                    tail = jnp.where(here, pltpu.roll(x, (SMAX * q + SMAX) % lanes, 1), tail)
+                    turned = pltpu.roll(x, SMAX * q, 1) if q else x
+                    head = jnp.where(lane // SMAX == q, turned, head)
+                    tail = jnp.where(lane // SMAX == (q + POLAR - 1) % POLAR, turned, tail)
                 lon_out[turn, 0, v] = head
                 lon_out[turn, 1, v] = tail
             zonal(turn, 0, True).start()
@@ -234,27 +238,34 @@
             old = get_prev(v, j)
             new = old + tend
             put(v, j, x + 0.1 * (old - 2.0 * x + new), new)
-
-        def plain(j, carry):
-            zu = -zcoef_ref[j] * src[0, j + 1]
-            mv = mcoef * src[1, j + 1]
-            pe = from_east[nvar]
-            pw = from_west[nvar]
-            for v in range(nvar):
-                x = src[v, j + 1]
-                place = v * rows + j
-                plus = jnp.where(
-                    lane == lanes - 1,
-                    pltpu.roll(pe, lanes - 1 - place, 1),
-                    pltpu.roll(x, lanes - 1, 1),
-                )
-                minus = jnp.where(
-                    lane == 0, pltpu.roll(pw, lax.rem(lanes - place, lanes), 1), pltpu.roll(x, 1, 1)
-                )
-                emit(v, j, x, plus - minus, plus + minus, zu, mv)
-            return carry
-
-        lax.fori_loop(body_lo, body_hi, plain, 0)
+            return new
+
+        halos = [
+            jnp.where(
+                lane % 2 == 0,
+                pltpu.roll(from_east[nvar + t], lanes - 1, 1),
+                pltpu.roll(from_west[nvar + t], 1, 1),
+            )
+            for t in range(tiles)
+        ]
+
+        def plain(group, edges):
+            for r in range(POLAR):
+                j = group * POLAR + r
+                zu = -zcoef_ref[j] * src[0, j + 1]
+                mv = mcoef * src[1, j + 1]
+                for v in range(nvar):
+                    x = src[v, j + 1]
+                    place = (v % per) * rows + j
+                    side = pltpu.roll(halos[v // per], lanes - 1 - 2 * place, 1)
+                    plus = jnp.where(lane == lanes - 1, side, pltpu.roll(x, lanes - 1, 1))
+                    minus = jnp.where(lane == 0, side, pltpu.roll(x, 1, 1))
+                    new = emit(v, j, x, plus - minus, plus + minus, zu, mv)
+                    if turn == 0:
+                        edges = packed(edges, v, j, new)
+            return edges
+
+        edges = lax.fori_loop(body_lo, body_hi, plain, no_edges if turn == 0 else ())
 
         @pl.when(polar)
         def _():
@@ -263,33 +274,40 @@
                 s = stride_ref[j]
                 m = flen_ref[j]
                 inv = 1.0 / jnp.full((lev, lanes), s, jnp.int32).astype(jnp.float32)
-                zu = (-zcoef_ref[j] * src[0, j + 1])
+                zu = -zcoef_ref[j] * src[0, j + 1]
                 mv = mcoef * src[1, j + 1]
                 for v in range(nvar):
                     x = src[v, j + 1]
-                    he = pltpu.roll(from_east[v], (lanes - SMAX * q) % lanes, 1)
-                    hw = pltpu.roll(from_west[v], (lanes - SMAX - SMAX * q) % lanes, 1)
+                    side = jnp.where(lane // SMAX == q, from_east[v], from_west[v])
+                    if q:
+                        side = pltpu.roll(side, lanes - SMAX * q, 1)
                     pair = []
                     for n in (s, m):
-                        plus = pltpu.roll(jnp.where(lane < n, he, x), lanes - n, 1)
-                        minus = pltpu.roll(jnp.where(lane >= lanes - n, hw, x), n, 1)
+                        plus = pltpu.roll(jnp.where(lane < n, side, x), lanes - n, 1)
+                        minus = pltpu.roll(jnp.where(lane >= lanes - n, side, x), n, 1)
                         pair.append((plus, minus))
                     diff = (pair[0][0] - pair[0][1]) * inv
                     emit(v, j, x, diff, pair[1][0] + pair[1][1], zu, mv)
 
-    def load(j, carry):
-        for v in range(nvar):
-            now0[v, j + 1] = now_ref[v, pl.ds(j, lev, stride=rows), :]
-        return carry
+        return edges
+
+    def load(group, edges):
+        for r in range(POLAR):
+            j = group * POLAR + r
+            for v in range(nvar):
+                x = now_ref[v, pl.ds(j, lev, stride=rows), :]
+                now0[v, j + 1] = x
+                edges = packed(edges, v, j, x)
+        return edges
 
     loads[1].wait()
-    lax.fori_loop(0, rows, load, 0)
+    edges = lax.fori_loop(0, rows // POLAR, load, no_edges)
     pl.semaphore_wait(
         barrier, 3 + jnp.where(lat > 0, 1, 0) + jnp.where(lat < n_lat - 1, 1, 0)
     )
 
     send_rows(0, now0)
-    send_sides(0, now0)
+    send_sides(0, now0, edges)
 
     for i in (*range(2, n_in), 0):
         loads[i].wait()
@@ -310,6 +328,16 @@
     bias2[...] = column(0.5 * b2_ref[...], 2 * lanes)
     bias3[...] = column(LOG2E * b3_ref[...], 2 * lanes)
     start3[...] = column(jnp.log2(band_ref[...]) * (-1.0 / RATE), 2 * lanes)
+    finish(0, now0)
+
+    def put_first(v, j, filtered, new):
+        prev1[v, j] = filtered
+        now1[v, j + 1] = new
+
+    edges = leap(0, now0, lambda v, j: prev_ref[v, pl.ds(j, lev, stride=rows), :], put_first)
+    send_rows(1, now1)
+    send_sides(1, now1, edges)
+
     half = list_ref.shape[1] // 2
     mine = count_ref[0, lon]
     other = count_ref[0, far]
@@ -331,15 +359,6 @@
             row_hot = (cols // lanes == j).astype(jnp.float32).astype(jnp.bfloat16)
             hot[pl.ds(j * lanes, lanes), at] = lane_hot * row_hot
 
-    finish(0, now0)
-
-    def put_first(v, j, filtered, new):
-        prev1[v, j] = filtered
-        now1[v, j + 1] = new
-
-    leap(0, now0, lambda v, j: prev_ref[v, pl.ds(j, lev, stride=rows), :], put_first)
-    send_rows(1, now1)
-    send_sides(1, now1)
     finish(1, now1)
 
     def put_second(v, j, filtered, new):
@@ -352,6 +371,13 @@
             now_out[v, pl.ds(j, lev, stride=rows), :] = new
 
     leap(1, now1, lambda v, j: prev1[v, j], put_second)
+
+    saves = [pltpu.make_async_copy(prev_out, prev_hbm, save_sem.at[0])]
+    for i, (a, b) in enumerate(((0, 2), (3, nvar), (2, 3))):
+        part = pl.ds(a, b - a)
+        saves.append(pltpu.make_async_copy(now_out.at[part], now_hbm.at[part], save_sem.at[i + 1]))
+    for save in saves[:3]:
+        save.start()
 
     wide = 2 * lanes
     chunk = 16
@@ -419,7 +445,7 @@
             heat[b, pl.ds(k, 1), :] = jnp.sum(above - total, axis=0, keepdims=True)
             return total
 
-        lax.fori_loop(0, lev, one_level, top, unroll=4)
+        lax.fori_loop(0, lev, one_level, top, unroll=8)
         back(b).start()
         return carry
 
@@ -445,6 +471,20 @@
     for j in range(rows):
         warm = grid[:, j * lanes : (j + 1) * lanes]
         now_out[2, pl.ds(j, lev, stride=rows), :] = temper[j] + warm
+    saves[3].start()
+    for save in saves:
+        save.wait()
+
+
+def hand_on(prev_ref, now_ref, prev_out, now_out, sem):
+    copies = []
+    for i, (src, dst) in enumerate(((prev_ref, prev_out), (now_ref, now_out))):
+        for v in range(src.shape[0]):
+            copies.append(pltpu.make_async_copy(src.at[v], dst.at[v], sem.at[i, v]))
+    for copy in copies:
+        copy.start()
+    for copy in copies:
+        copy.wait()
 
 
 def body(
@@ -473,7 +513,9 @@
     half = sunlit_cols.size // 2
     wide = 2 * lanes
     blocks = half // wide
-    vmem = pl.BlockSpec(memory_space=pltpu.VMEM)
+    tiles = -(-nvar // (lanes // 2 // rows))
+    hbm = pl.BlockSpec(memory_space=pltpu.HBM)
+    limit = 63 * 1024 * 1024
     f32, bf16 = jnp.float32, jnp.bfloat16
     tile = (lev, lanes)
     shape = jax.ShapeDtypeStruct(flat, f32)
@@ -499,17 +541,19 @@
     prev, now = pl.pallas_call(
         functools.partial(kernel, dims, len(operands)),
         out_shape=(shape, shape),
-        in_specs=[pl.BlockSpec(memory_space=pltpu.HBM)] * len(operands),
-        out_specs=(vmem, vmem),
+        in_specs=[hbm] * len(operands),
+        out_specs=(hbm, hbm),
         scratch_shapes=[space(x.shape, x.dtype) for space, x in zip(spaces, operands)]
         + [
+            pltpu.VMEM(flat, f32),
+            pltpu.VMEM(flat, f32),
             pltpu.VMEM((nvar, rows + 2) + tile, f32),
             pltpu.VMEM((nvar, rows + 2) + tile, f32),
             pltpu.VMEM((nvar, rows) + tile, f32),
             pltpu.VMEM((rows,) + tile, f32),
             pltpu.VMEM((nvar * lev, rows * lanes), bf16),
-            pltpu.VMEM((2, 2, nvar + 1) + tile, f32),
-            pltpu.VMEM((2, 2, nvar + 1) + tile, f32),
+            pltpu.VMEM((2, 2, nvar + tiles) + tile, f32),
+            pltpu.VMEM((2, 2, nvar + tiles) + tile, f32),
             pltpu.VMEM((2, 2, nvar) + tile, f32),
             pltpu.VMEM((lev * hid, nvar * lev), bf16),
             pltpu.VMEM((hid, hid), bf16),
@@ -529,15 +573,24 @@
             pltpu.VMEM((blocks, lev, wide), f32),
             pltpu.VMEM((lev, rows * lanes), f32),
             pltpu.SemaphoreType.DMA((len(operands),)),
+            pltpu.SemaphoreType.DMA((4,)),
             pltpu.SemaphoreType.DMA((2, 4)),
             pltpu.SemaphoreType.DMA((2, 4)),
             pltpu.SemaphoreType.DMA((2, blocks)),
             pltpu.SemaphoreType.DMA((2, blocks)),
         ],
         compiler_params=pltpu.CompilerParams(
-            collective_id=0, has_side_effects=True, vmem_limit_bytes=63 * 1024 * 1024
+            collective_id=0, has_side_effects=True, vmem_limit_bytes=limit
         ),
     )(*operands)
+    prev, now = pl.pallas_call(
+        hand_on,
+        out_shape=(shape, shape),
+        in_specs=[hbm, hbm],
+        out_specs=(hbm, hbm),
+        scratch_shapes=[pltpu.SemaphoreType.DMA((2, nvar))],
+        compiler_params=pltpu.CompilerParams(vmem_limit_bytes=limit),
+    )(prev, now)
     return prev.reshape(state_prev.shape), now.reshape(state_now.shape)
 
 

time: 41.5 us -> 91.9 us (2.21)
  Pallas kernels: 37.5 us -> 91.1 us
  local copies, waits for them, and re-layouts: 3.19 us -> 0 us
    pallas_call x0 -> x1, Pallas kernels: none -> 56.8 us  [body(): pl.pallas_call(hand_on, out_shape=(shape, shape), in_specs=[hbm, hbm], ou...]
    pallas_call x1, Pallas kernels: 37.5 us -> 34.3 us  [body(): pl.pallas_call(functools.partial(kernel, dims, len(operands)), out_shape=...]
    unnamed x4 -> x0, local copies, waits for them, and re-layouts: 3.19 us -> none
where the time goes in v3:
time: 91.9 us; the launch traced here: 91.8 us
  Pallas kernels  91.1 us (99%)
    pallas_call x1, Pallas kernels, body(): pl.pallas_call(hand_on, out_shape=(shape, shape), in_specs=[hbm, hbm], ou...  56.8 us
    pallas_call x1, Pallas kernels, body(): pl.pallas_call(functools.partial(kernel, dims, len(operands)), out_shape=...  34.3 us

profile of v3, /device:TPU:0, one launch (start us, length us, event | category | flops | bytes accessed | tf_op | source)
XLA Modules:
  0.0 91.8 jit_solution(18322142991412679843)
XLA Ops:
  0.6 34.3 %shard_map.167 = (f32[7,256,128]{2,1,0:T(8,128)}, f32[7,256,128]{2,1,0:T(8,128)}) custom-call(f32[7,256,128]{2,1,0:T(8,128)} %bitcast.11, f32[7,256,128]{2,1,0:T(8,128)} %bitcast.12, s32[16]{0:T(128)} %refs_2_.1, s32[16]{0:T(128)} %refs_3_.1, f32[16]{0:T(128)} %refs_4_.1, s32[1,8]{1,0:T(1,128)} %refs_5_.1, f32[1,16]{1,0:T(1,128)} %bitcast.16, ...), custom_call_target="tpu_custom_call" | custom-call | tf_op jit(solution)/shard_map/pallas_call | solution.py:541
  34.9 56.8 %shard_map.168 = (f32[7,256,128]{2,1,0:T(8,128)}, f32[7,256,128]{2,1,0:T(8,128)}) custom-call(f32[7,256,128]{2,1,0:T(8,128)} %get-tuple-element.6.prev_ref, f32[7,256,128]{2,1,0:T(8,128)} %get-tuple-element.7.now_ref), custom_call_target="tpu_custom_call" | custom-call | tf_op jit(solution)/shard_map/pallas_call | solution.py:586

commit v4 on v3

--- a/solution.py
+++ b/solution.py
@@ -99,8 +99,6 @@
     at_end = lat == n_lat - 1
     polar = jnp.logical_or(at_top, at_end)
     pstart = jnp.where(at_top, 0, rows - POLAR)
-    body_lo = jnp.where(at_top, 1, 0)
-    body_hi = jnp.where(at_end, rows // POLAR - 1, rows // POLAR)
     per = lanes // 2 // rows
     tiles = -(-nvar // per)
 
@@ -125,13 +123,13 @@
 
     lane = lax.broadcasted_iota(jnp.int32, (lev, lanes), 1)
 
-    def zonal(turn, side, whole):
-        part = pl.ds(0, nvar + tiles) if whole else pl.ds(nvar, tiles)
+    def zonal(turn, side, kind):
+        part = pl.ds(nvar, tiles) if kind else pl.ds(0, nvar)
         return pltpu.make_async_remote_copy(
             src_ref=lon_out.at[turn, side, part],
             dst_ref=lon_in.at[turn, side, part],
-            send_sem=send_sem.at[turn, side],
-            recv_sem=recv_sem.at[turn, side],
+            send_sem=send_sem.at[turn, 2 * kind + side],
+            recv_sem=recv_sem.at[turn, 2 * kind + side],
             device_id={"lon": west if side == 0 else east},
             device_id_type=MESH,
         )
@@ -140,8 +138,8 @@
         return pltpu.make_async_remote_copy(
             src_ref=src.at[:, 1 if side == 0 else rows],
             dst_ref=lat_in.at[turn, side],
-            send_sem=send_sem.at[turn, 2 + side],
-            recv_sem=recv_sem.at[turn, 2 + side],
+            send_sem=send_sem.at[turn, 4 + side],
+            recv_sem=recv_sem.at[turn, 4 + side],
             device_id={"lat": lat - 1 if side == 0 else lat + 1},
             device_id_type=MESH,
         )
@@ -164,41 +162,53 @@
 
     no_edges = (jnp.zeros((lev, lanes), jnp.float32),) * tiles
 
-    def send_sides(turn, src, edges):
+    def send_polar(turn, src):
+        for v in range(nvar):
+            head = jnp.zeros((lev, lanes), jnp.float32)
+            tail = head
+            for q in range(POLAR):
+                x = src[v, pstart + q + 1]
+                turned = pltpu.roll(x, SMAX * q, 1) if q else x
+                head = jnp.where(lane // SMAX == q, turned, head)
+                tail = jnp.where(lane // SMAX == (q + POLAR - 1) % POLAR, turned, tail)
+            lon_out[turn, 0, v] = head
+            lon_out[turn, 1, v] = tail
+        zonal(turn, 0, 0).start()
+        zonal(turn, 1, 0).start()
+
+    def send_early(turn, src):
+        send_rows(turn, src)
+
+        @pl.when(polar)
+        def _():
+            send_polar(turn, src)
+
+    def send_edges(turn):
+        for t in range(tiles):
+            lon_out[turn, 1, nvar + t] = lon_out[turn, 0, nvar + t]
+        zonal(turn, 0, 1).start()
+        zonal(turn, 1, 1).start()
+
+    groups = rows // POLAR
+
+    def group_at(i):
+        return jnp.where(i == 0, 0, jnp.where(i == 1, groups - 1, i - 1))
+
+    def held_edges(turn):
+        return tuple(lon_out[turn, 0, nvar + t] for t in range(tiles))
+
+    def hold_edges(turn, edges):
         for t in range(tiles):
             lon_out[turn, 0, nvar + t] = edges[t]
-            lon_out[turn, 1, nvar + t] = edges[t]
+
+    def finish(turn, src):
+        zonal(turn, 0, 1).wait()
+        zonal(turn, 1, 1).wait()
 
         @pl.when(polar)
         def _():
-            for v in range(nvar):
-                head = jnp.zeros((lev, lanes), jnp.float32)
-                tail = head
-                for q in range(POLAR):
-                    x = src[v, pstart + q + 1]
-                    turned = pltpu.roll(x, SMAX * q, 1) if q else x
-                    head = jnp.where(lane // SMAX == q, turned, head)
-                    tail = jnp.where(lane // SMAX == (q + POLAR - 1) % POLAR, turned, tail)
-                lon_out[turn, 0, v] = head
-                lon_out[turn, 1, v] = tail
-            zonal(turn, 0, True).start()
-            zonal(turn, 1, True).start()
-
-        @pl.when(jnp.logical_not(polar))
-        def _():
-            zonal(turn, 0, False).start()
-            zonal(turn, 1, False).start()
-
-    def finish(turn, src):
-        @pl.when(polar)
-        def _():
-            zonal(turn, 0, True).wait()
-            zonal(turn, 1, True).wait()
-
-        @pl.when(jnp.logical_not(polar))
-        def _():
-            zonal(turn, 0, False).wait()
-            zonal(turn, 1, False).wait()
+            zonal(turn, 0, 0).wait()
+            zonal(turn, 1, 0).wait()
 
         @pl.when(lat > 0)
         def _():
@@ -249,7 +259,8 @@
             for t in range(tiles)
         ]
 
-        def plain(group, edges):
+        def plain(group):
+            edges = held_edges(1) if turn == 0 else ()
             for r in range(POLAR):
                 j = group * POLAR + r
                 zu = -zcoef_ref[j] * src[0, j + 1]
@@ -263,9 +274,8 @@
                     new = emit(v, j, x, plus - minus, plus + minus, zu, mv)
                     if turn == 0:
                         edges = packed(edges, v, j, new)
-            return edges
-
-        edges = lax.fori_loop(body_lo, body_hi, plain, no_edges if turn == 0 else ())
+            if turn == 0:
+                hold_edges(1, edges)
 
         @pl.when(polar)
         def _():
@@ -289,25 +299,53 @@
                     diff = (pair[0][0] - pair[0][1]) * inv
                     emit(v, j, x, diff, pair[1][0] + pair[1][1], zu, mv)
 
-        return edges
-
-    def load(group, edges):
+        def one_group(i, carry):
+            group = group_at(i)
+            skip = jnp.logical_or(
+                jnp.logical_and(at_top, group == 0), jnp.logical_and(at_end, group == groups - 1)
+            )
+
+            @pl.when(jnp.logical_not(skip))
+            def _():
+                plain(group)
+
+            if turn == 0:
+
+                @pl.when(i == 1)
+                def _():
+                    send_early(1, now1)
+
+            return carry
+
+        if turn == 0:
+            hold_edges(1, no_edges)
+        lax.fori_loop(0, groups, one_group, 0)
+
+    def load(i, carry):
+        group = group_at(i)
+        edges = held_edges(0)
         for r in range(POLAR):
             j = group * POLAR + r
             for v in range(nvar):
                 x = now_ref[v, pl.ds(j, lev, stride=rows), :]
                 now0[v, j + 1] = x
                 edges = packed(edges, v, j, x)
-        return edges
-
+        hold_edges(0, edges)
+
+        @pl.when(i == 1)
+        def _():
+            send_early(0, now0)
+
+        return carry
+
+    hold_edges(0, no_edges)
     loads[1].wait()
-    edges = lax.fori_loop(0, rows // POLAR, load, no_edges)
     pl.semaphore_wait(
         barrier, 3 + jnp.where(lat > 0, 1, 0) + jnp.where(lat < n_lat - 1, 1, 0)
     )
 
-    send_rows(0, now0)
-    send_sides(0, now0, edges)
+    lax.fori_loop(0, groups, load, 0)
+    send_edges(0)
 
     for i in (*range(2, n_in), 0):
         loads[i].wait()
@@ -321,8 +359,8 @@
     )
     level = lax.broadcasted_iota(jnp.int32, (hid, nvar * lev), 1) % lev
     for k in range(lev):
-        w1big[pl.ds(k * hid, hid), :] = jnp.where(level == k, spread, 0.0).astype(jnp.bfloat16)
-    w2t[...] = flipped(w2_ref[...]).astype(jnp.bfloat16)
+        w1big[pl.ds(k * hid, hid), :] = jnp.where(level == k, 0.5 * spread, 0.0).astype(jnp.bfloat16)
+    w2t[...] = (0.5 * flipped(w2_ref[...])).astype(jnp.bfloat16)
     w3t[...] = flipped(w3_ref[...]).astype(jnp.bfloat16)
     bias1[...] = column(0.5 * b1_ref[...], 2 * lanes)
     bias2[...] = column(0.5 * b2_ref[...], 2 * lanes)
@@ -334,9 +372,8 @@
         prev1[v, j] = filtered
         now1[v, j + 1] = new
 
-    edges = leap(0, now0, lambda v, j: prev_ref[v, pl.ds(j, lev, stride=rows), :], put_first)
-    send_rows(1, now1)
-    send_sides(1, now1, edges)
+    leap(0, now0, lambda v, j: prev_ref[v, pl.ds(j, lev, stride=rows), :], put_first)
+    send_edges(1)
 
     half = list_ref.shape[1] // 2
     mine = count_ref[0, lon]
@@ -418,11 +455,11 @@
         cells = own[b] + come[b]
         for k in range(lev):
             part = pl.ds(k * hid, hid)
-            x = 0.5 * jnp.dot(w1big[part, :], cells, preferred_element_type=jnp.float32) + bias1[...]
+            x = jnp.dot(w1big[part, :], cells, preferred_element_type=jnp.float32) + bias1[...]
             first[part, :] = (x + x * jnp.tanh(x)).astype(jnp.bfloat16)
         for k in range(lev):
             part = pl.ds(k * hid, hid)
-            x = 0.5 * jnp.dot(w2t[...], first[part, :], preferred_element_type=jnp.float32) + bias2[...]
+            x = jnp.dot(w2t[...], first[part, :], preferred_element_type=jnp.float32) + bias2[...]
             second[part, :] = (x + x * jnp.tanh(x)).astype(jnp.bfloat16)
         depth[...] = start3[...]
         top = jnp.zeros((8, wide), jnp.float32)
@@ -430,7 +467,7 @@
             top = top + jnp.exp2(-RATE * start3[pl.ds(g, 8), :])
 
         def one_level(k, above):
-            part = pl.ds(pl.multiple_of(k * hid, hid), hid)
+            part = pl.ds(k * hid, hid)
             raw = jnp.dot(w3t[...], second[part, :], preferred_element_type=jnp.float32)
             total = jnp.zeros((8, wide), jnp.float32)
             for g in range(0, gpt, chunk):
@@ -445,7 +482,9 @@
             heat[b, pl.ds(k, 1), :] = jnp.sum(above - total, axis=0, keepdims=True)
             return total
 
-        lax.fori_loop(0, lev, one_level, top, unroll=8)
+        above = top
+        for k in range(lev):
+            above = one_level(k, above)
         back(b).start()
         return carry
 
@@ -476,15 +515,19 @@
         save.wait()
 
 
-def hand_on(prev_ref, now_ref, prev_out, now_out, sem):
-    copies = []
+def hand_on(prev_ref, now_ref, prev_out, now_out, stage, sem):
+    ins, outs = [], []
     for i, (src, dst) in enumerate(((prev_ref, prev_out), (now_ref, now_out))):
         for v in range(src.shape[0]):
-            copies.append(pltpu.make_async_copy(src.at[v], dst.at[v], sem.at[i, v]))
-    for copy in copies:
+            ins.append(pltpu.make_async_copy(src.at[v], stage.at[i, v], sem.at[0, i, v]))
+            outs.append(pltpu.make_async_copy(stage.at[i, v], dst.at[v], sem.at[1, i, v]))
+    for copy in ins:
         copy.start()
-    for copy in copies:
+    for copy, out in zip(ins, outs):
         copy.wait()
+        out.start()
+    for out in outs:
+        out.wait()
 
 
 def body(
@@ -574,8 +617,8 @@
             pltpu.VMEM((lev, rows * lanes), f32),
             pltpu.SemaphoreType.DMA((len(operands),)),
             pltpu.SemaphoreType.DMA((4,)),
-            pltpu.SemaphoreType.DMA((2, 4)),
-            pltpu.SemaphoreType.DMA((2, 4)),
+            pltpu.SemaphoreType.DMA((2, 6)),
+            pltpu.SemaphoreType.DMA((2, 6)),
             pltpu.SemaphoreType.DMA((2, blocks)),
             pltpu.SemaphoreType.DMA((2, blocks)),
         ],
@@ -588,7 +631,7 @@
         out_shape=(shape, shape),
         in_specs=[hbm, hbm],
         out_specs=(hbm, hbm),
-        scratch_shapes=[pltpu.SemaphoreType.DMA((2, nvar))],
+        scratch_shapes=[pltpu.VMEM((2,) + flat, f32), pltpu.SemaphoreType.DMA((2, 2, nvar))],
         compiler_params=pltpu.CompilerParams(vmem_limit_bytes=limit),
     )(prev, now)
     return prev.reshape(state_prev.shape), now.reshape(state_now.shape)

time: 91.9 us -> 36 us (0.39)
  Pallas kernels: 91.1 us -> 35.2 us
    pallas_call x1, Pallas kernels: 56.8 us -> 2.45 us  [body(): pl.pallas_call(hand_on, out_shape=(shape, shape), in_specs=[hbm, hbm], ou...]
    pallas_call x1, Pallas kernels: 34.3 us -> 32.7 us  [body(): pl.pallas_call(functools.partial(kernel, dims, len(operands)), out_shape=...]
where the time goes in v4:
time: 36 us; the launch traced here: 35.8 us
  Pallas kernels  35.2 us (98%)
  between operations  0.64 us (2%)
    pallas_call x1, Pallas kernels, body(): pl.pallas_call(functools.partial(kernel, dims, len(operands)), out_shape=...  32.7 us
    pallas_call x1, Pallas kernels, body(): pl.pallas_call(hand_on, out_shape=(shape, shape), in_specs=[hbm, hbm], ou...  2.45 us

profile of v4, /device:TPU:0, one launch (start us, length us, event | category | flops | bytes accessed | tf_op | source)
XLA Modules:
  0.0 35.8 jit_solution(7571642401571703392)
XLA Ops:
  0.6 32.7 %shard_map.167 = (f32[7,256,128]{2,1,0:T(8,128)}, f32[7,256,128]{2,1,0:T(8,128)}) custom-call(f32[7,256,128]{2,1,0:T(8,128)} %bitcast.11, f32[7,256,128]{2,1,0:T(8,128)} %bitcast.12, s32[16]{0:T(128)} %refs_2_.1, s32[16]{0:T(128)} %refs_3_.1, f32[16]{0:T(128)} %refs_4_.1, s32[1,8]{1,0:T(1,128)} %refs_5_.1, f32[1,16]{1,0:T(1,128)} %bitcast.16, ...), custom_call_target="tpu_custom_call" | custom-call | tf_op jit(solution)/shard_map/pallas_call | solution.py:584
  33.4 2.5 %shard_map.168 = (f32[7,256,128]{2,1,0:T(8,128)}, f32[7,256,128]{2,1,0:T(8,128)}) custom-call(f32[7,256,128]{2,1,0:T(8,128)} %get-tuple-element.6.prev_ref, f32[7,256,128]{2,1,0:T(8,128)} %get-tuple-element.7.now_ref), custom_call_target="tpu_custom_call" | custom-call | tf_op jit(solution)/shard_map/pallas_call | solution.py:629

commit v5 on v4

--- a/solution.py
+++ b/solution.py
@@ -13,6 +13,7 @@
 MESH = pl.DeviceIdType.MESH
 LOG2E = math.log2(math.e)
 RATE = 0.15
+FALL = -RATE * LOG2E
 
 
 def column(row, lanes):
@@ -362,10 +363,11 @@
         w1big[pl.ds(k * hid, hid), :] = jnp.where(level == k, 0.5 * spread, 0.0).astype(jnp.bfloat16)
     w2t[...] = (0.5 * flipped(w2_ref[...])).astype(jnp.bfloat16)
     w3t[...] = flipped(w3_ref[...]).astype(jnp.bfloat16)
-    bias1[...] = column(0.5 * b1_ref[...], 2 * lanes)
-    bias2[...] = column(0.5 * b2_ref[...], 2 * lanes)
-    bias3[...] = column(LOG2E * b3_ref[...], 2 * lanes)
-    start3[...] = column(jnp.log2(band_ref[...]) * (-1.0 / RATE), 2 * lanes)
+    bias1[...] = column(0.5 * b1_ref[...], lanes)
+    bias2[...] = column(0.5 * b2_ref[...], lanes)
+    bias3[...] = column(b3_ref[...], lanes)
+    start3[...] = column(jnp.log(band_ref[...]) * (-1.0 / RATE), lanes)
+
     finish(0, now0)
 
     def put_first(v, j, filtered, new):
@@ -419,6 +421,10 @@
     wide = 2 * lanes
     chunk = 16
     blocks = half // wide
+    merge = math.gcd(lev, 4)
+
+    def doubled(x):
+        return jnp.concatenate([x, x], axis=1)
 
     def picked(at):
         got = jnp.dot(feats[...], hot[:, pl.ds(at, wide)], preferred_element_type=jnp.float32)
@@ -453,18 +459,24 @@
     def absorb(b, carry):
         to_far(b).wait()
         cells = own[b] + come[b]
+        shift1 = doubled(bias1[...])
+        shift2 = doubled(bias2[...])
+        for k in range(0, lev, merge):
+            raw = jnp.dot(
+                w1big[pl.ds(k * hid, merge * hid), :], cells, preferred_element_type=jnp.float32
+            )
+            for i in range(merge):
+                x = raw[i * hid : (i + 1) * hid] + shift1
+                first[pl.ds((k + i) * hid, hid), :] = (x + x * jnp.tanh(x)).astype(jnp.bfloat16)
         for k in range(lev):
             part = pl.ds(k * hid, hid)
-            x = jnp.dot(w1big[part, :], cells, preferred_element_type=jnp.float32) + bias1[...]
-            first[part, :] = (x + x * jnp.tanh(x)).astype(jnp.bfloat16)
-        for k in range(lev):
-            part = pl.ds(k * hid, hid)
-            x = jnp.dot(w2t[...], first[part, :], preferred_element_type=jnp.float32) + bias2[...]
+            x = jnp.dot(w2t[...], first[part, :], preferred_element_type=jnp.float32) + shift2
             second[part, :] = (x + x * jnp.tanh(x)).astype(jnp.bfloat16)
-        depth[...] = start3[...]
-        top = jnp.zeros((8, wide), jnp.float32)
+        depth[...] = doubled(start3[...])
+        top = jnp.zeros((8, lanes), jnp.float32)
         for g in range(0, gpt, 8):
-            top = top + jnp.exp2(-RATE * start3[pl.ds(g, 8), :])
+            top = top + jnp.exp2(FALL * start3[pl.ds(g, 8), :])
+        top = doubled(top)
 
         def one_level(k, above):
             part = pl.ds(k * hid, hid)
@@ -472,11 +484,11 @@
             total = jnp.zeros((8, wide), jnp.float32)
             for g in range(0, gpt, chunk):
                 at = pl.ds(g, chunk)
-                y = raw[g : g + chunk] * LOG2E + bias3[at, :]
-                soft = jnp.maximum(y, jnp.log2(1.0 + jnp.exp2(jnp.minimum(y, 64.0))))
+                x = raw[g : g + chunk] + doubled(bias3[at, :])
+                soft = jnp.maximum(x, jnp.log(1.0 + jnp.exp(jnp.minimum(x, 44.0))))
                 here = depth[at, :] + soft
                 depth[at, :] = here
-                left = jnp.exp2(-RATE * here)
+                left = jnp.exp2(FALL * here)
                 for piece in range(0, chunk, 8):
                     total = total + left[piece : piece + 8]
             heat[b, pl.ds(k, 1), :] = jnp.sum(above - total, axis=0, keepdims=True)
@@ -497,16 +509,19 @@
         low = (rest - mid.astype(jnp.float32)).astype(jnp.bfloat16)
         out = lax.dot_general(
             jnp.concatenate([high, mid, low], axis=0),
-            hot[:, pl.ds(at, half)],
+            hot[:, pl.ds(at, wide)],
             (((1,), (1,)), ((), ())),
             preferred_element_type=jnp.float32,
         )
         return out[:lev] + out[lev : 2 * lev] + out[2 * lev :]
 
-    grid[...] = placed(jnp.concatenate([heat[b] for b in range(blocks)], axis=1), 0)
+    total = placed(heat[0], 0)
+    for b in range(1, blocks):
+        total = total + placed(heat[b], b * wide)
+    grid[...] = total
     for b in range(blocks):
         back(b).wait()
-    grid[...] += placed(jnp.concatenate([heat_in[b] for b in range(blocks)], axis=1), half)
+        grid[...] += placed(heat_in[b], half + b * wide)
     for j in range(rows):
         warm = grid[:, j * lanes : (j + 1) * lanes]
         now_out[2, pl.ds(j, lev, stride=rows), :] = temper[j] + warm
@@ -601,10 +616,10 @@
             pltpu.VMEM((lev * hid, nvar * lev), bf16),
             pltpu.VMEM((hid, hid), bf16),
             pltpu.VMEM((gpt, hid), bf16),
-            pltpu.VMEM((hid, wide), f32),
-            pltpu.VMEM((hid, wide), f32),
-            pltpu.VMEM((gpt, wide), f32),
-            pltpu.VMEM((gpt, wide), f32),
+            pltpu.VMEM((hid, lanes), f32),
+            pltpu.VMEM((hid, lanes), f32),
+            pltpu.VMEM((gpt, lanes), f32),
+            pltpu.VMEM((gpt, lanes), f32),
             pltpu.VMEM((lev * hid, wide), bf16),
             pltpu.VMEM((lev * hid, wide), bf16),
             pltpu.VMEM((gpt, wide), f32),

time: 36 us -> 35.5 us (0.986)
  Pallas kernels: 35.2 us -> 34.7 us
    pallas_call x1, Pallas kernels: 32.7 us -> 32.2 us  [body(): pl.pallas_call(functools.partial(kernel, dims, len(operands)), out_shape=...]
where the time goes in v5:
time: 35.5 us; the launch traced here: 35.3 us
  Pallas kernels  34.7 us (98%)
  between operations  0.64 us (2%)
    pallas_call x1, Pallas kernels, body(): pl.pallas_call(functools.partial(kernel, dims, len(operands)), out_shape=...  32.2 us
    pallas_call x1, Pallas kernels, body(): pl.pallas_call(hand_on, out_shape=(shape, shape), in_specs=[hbm, hbm], ou...  2.45 us

profile of v5, /device:TPU:0, one launch (start us, length us, event | category | flops | bytes accessed | tf_op | source)
XLA Modules:
  0.0 35.3 jit_solution(3123527412366161453)
XLA Ops:
  0.6 32.2 %shard_map.167 = (f32[7,256,128]{2,1,0:T(8,128)}, f32[7,256,128]{2,1,0:T(8,128)}) custom-call(f32[7,256,128]{2,1,0:T(8,128)} %bitcast.11, f32[7,256,128]{2,1,0:T(8,128)} %bitcast.12, s32[16]{0:T(128)} %refs_2_.1, s32[16]{0:T(128)} %refs_3_.1, f32[16]{0:T(128)} %refs_4_.1, s32[1,8]{1,0:T(1,128)} %refs_5_.1, f32[1,16]{1,0:T(1,128)} %bitcast.16, ...), custom_call_target="tpu_custom_call" | custom-call | tf_op jit(solution)/shard_map/pallas_call | solution.py:599
  32.9 2.5 %shard_map.168 = (f32[7,256,128]{2,1,0:T(8,128)}, f32[7,256,128]{2,1,0:T(8,128)}) custom-call(f32[7,256,128]{2,1,0:T(8,128)} %get-tuple-element.6.prev_ref, f32[7,256,128]{2,1,0:T(8,128)} %get-tuple-element.7.now_ref), custom_call_target="tpu_custom_call" | custom-call | tf_op jit(solution)/shard_map/pallas_call | solution.py:644

commit v6 on v5

--- a/solution.py
+++ b/solution.py
@@ -533,9 +533,10 @@
 def hand_on(prev_ref, now_ref, prev_out, now_out, stage, sem):
     ins, outs = [], []
     for i, (src, dst) in enumerate(((prev_ref, prev_out), (now_ref, now_out))):
-        for v in range(src.shape[0]):
-            ins.append(pltpu.make_async_copy(src.at[v], stage.at[i, v], sem.at[0, i, v]))
-            outs.append(pltpu.make_async_copy(stage.at[i, v], dst.at[v], sem.at[1, i, v]))
+        cut = src.shape[0] // 2
+        for v, part in enumerate((pl.ds(0, cut), pl.ds(cut, src.shape[0] - cut))):
+            ins.append(pltpu.make_async_copy(src.at[part], stage.at[i, part], sem.at[0, i, v]))
+            outs.append(pltpu.make_async_copy(stage.at[i, part], dst.at[part], sem.at[1, i, v]))
     for copy in ins:
         copy.start()
     for copy, out in zip(ins, outs):
@@ -646,7 +647,7 @@
         out_shape=(shape, shape),
         in_specs=[hbm, hbm],
         out_specs=(hbm, hbm),
-        scratch_shapes=[pltpu.VMEM((2,) + flat, f32), pltpu.SemaphoreType.DMA((2, 2, nvar))],
+        scratch_shapes=[pltpu.VMEM((2,) + flat, f32), pltpu.SemaphoreType.DMA((2, 2, 2))],
         compiler_params=pltpu.CompilerParams(vmem_limit_bytes=limit),
     )(prev, now)
     return prev.reshape(state_prev.shape), now.reshape(state_now.shape)

time: 35.5 us -> 35.4 us (level)
  no operation moved by 1% of the time
where the time goes in v6:
time: 35.4 us; the launch traced here: 35.2 us
  Pallas kernels  34.6 us (98%)
  between operations  0.64 us (2%)
    pallas_call x1, Pallas kernels, body(): pl.pallas_call(functools.partial(kernel, dims, len(operands)), out_shape=...  32.2 us
    pallas_call x1, Pallas kernels, body(): pl.pallas_call(hand_on, out_shape=(shape, shape), in_specs=[hbm, hbm], ou...  2.33 us

profile of v6, /device:TPU:0, one launch (start us, length us, event | category | flops | bytes accessed | tf_op | source)
XLA Modules:
  0.0 35.2 jit_solution(18110207840005132734)
XLA Ops:
  0.6 32.2 %shard_map.167 = (f32[7,256,128]{2,1,0:T(8,128)}, f32[7,256,128]{2,1,0:T(8,128)}) custom-call(f32[7,256,128]{2,1,0:T(8,128)} %bitcast.11, f32[7,256,128]{2,1,0:T(8,128)} %bitcast.12, s32[16]{0:T(128)} %refs_2_.1, s32[16]{0:T(128)} %refs_3_.1, f32[16]{0:T(128)} %refs_4_.1, s32[1,8]{1,0:T(1,128)} %refs_5_.1, f32[1,16]{1,0:T(1,128)} %bitcast.16, ...), custom_call_target="tpu_custom_call" | custom-call | tf_op jit(solution)/shard_map/pallas_call | solution.py:600
  32.9 2.3 %shard_map.168 = (f32[7,256,128]{2,1,0:T(8,128)}, f32[7,256,128]{2,1,0:T(8,128)}) custom-call(f32[7,256,128]{2,1,0:T(8,128)} %get-tuple-element.6.prev_ref, f32[7,256,128]{2,1,0:T(8,128)} %get-tuple-element.7.now_ref), custom_call_target="tpu_custom_call" | custom-call | tf_op jit(solution)/shard_map/pallas_call | solution.py:645
